TPU v7x, 32 devices: a whole 2x2x4 slice. The times are simulated.
32 devices in a mesh: section: 4 (over y, x), band: 4 (over z), members: 2 (over core).
Axes of the slice: x: 2, y: 2, z: 4, core: 2. Of those that a mesh axis runs over, the one named last changes fastest.
Arguments:
- fields: bfloat16 [8, 16, 576, 128], P(('members', 'section'), 'band'), parts along dimension 0, may hold values from -6 to 6
- lat_taps: bfloat16 [2, 9, 128], replicated, may hold values from -1.5 to 1.5
- lon_taps: bfloat16 [2, 9, 128], replicated, may hold values from -1.5 to 1.5
- gains: float32 [2, 128], replicated, may hold values from 0.1 to 1.9
- w_in: bfloat16 [2, 128, 256], replicated, may hold values from -0.5 to 0.5
- w_out: bfloat16 [2, 256, 128], replicated, may hold values from -0.375 to 0.375
Outputs:
- final_states: bfloat16 [8, 16, 576, 128], P(('members', 'section'), 'band'), parts along dimension 0
There are 2 independent parts, one for each index of `members`. A program takes and returns all parts, laid end to end along the dimension named above; an argument that names none is the same for every part. Nothing has to cross between parts.
All inputs are finite; a program needn't handle non-finite values.
Results may differ from a plain program's by a relative error of at most 0.0063.
Values may be sent and summed in bfloat16 or wider, within the bound.
No kernel may reach another device: no remote copies, remote signals or barrier semaphores. Data moves between devices by JAX's collectives and lax.ppermute only.
A program may use at most 64 MiB of HBM per device.

v0:
```python
import jax
import jax.numpy as jnp
from jax import lax
from jax.sharding import PartitionSpec as P

DLON = 3
LAYERS = 2


def column_mix(padded, lat_w, rows):
    lat_tap = lat_w.astype(jnp.float32)
    total = jnp.zeros(padded.shape[:1] + (rows,) + padded.shape[2:], jnp.float32)
    for k in range(9):
        total = total + padded[:, k : k + rows].astype(jnp.float32) * lat_tap[k]
    return total.astype(jnp.bfloat16)


def layer_rest(state, latmix, lon_w, gain, proj_in, proj_out):
    lon_tap = lon_w.astype(jnp.float32)
    lonmix = jnp.zeros(latmix.shape, jnp.float32)
    for k in range(9):
        lonmix = lonmix + jnp.roll(latmix, -DLON * (k - 4), axis=2).astype(jnp.float32) * lon_tap[k]
    mean = jnp.mean(lonmix, axis=-1, keepdims=True)
    centred = lonmix - mean
    var = jnp.mean(centred * centred, axis=-1, keepdims=True)
    normed = (centred / jnp.sqrt(var + 1e-06) * gain).astype(jnp.bfloat16)
    flat = normed.reshape(-1, normed.shape[-1])
    hidden = jax.nn.gelu(
        jnp.dot(flat, proj_in, preferred_element_type=jnp.float32), approximate=False
    ).astype(jnp.bfloat16)
    delta = jnp.dot(hidden, proj_out, preferred_element_type=jnp.float32).reshape(latmix.shape)
    return (state.astype(jnp.float32) + delta).astype(jnp.bfloat16)


def shards(fields, lat_taps, lon_taps, gains, w_in, w_out):
    state = fields
    for layer in range(LAYERS):
        lat_w = lat_taps[layer]
        columns = lax.all_to_all(state, "band", split_axis=2, concat_axis=1, tiled=True)
        padded = jnp.pad(columns, ((0, 0), (4, 4), (0, 0), (0, 0)))
        mixed = column_mix(padded, lat_w, columns.shape[1])
        latmix = lax.all_to_all(mixed, "band", split_axis=1, concat_axis=2, tiled=True)
        state = layer_rest(state, latmix, lon_taps[layer], gains[layer], w_in[layer], w_out[layer])
    return state


def solution(mesh):
    return jax.shard_map(
        shards,
        mesh=mesh,
        in_specs=(P(("members", "section"), "band", None, None), P(), P(), P(), P(), P()),
        out_specs=P(("members", "section"), "band", None, None),
        check_vma=False,
    )
```

profile of v0, /device:TPU:0, one launch (start us, length us, event | category | flops | bytes accessed | tf_op | source)
XLA Modules:
  0.0 128.4 jit_solution(2488933299521540204)
XLA Ops:
  0.0 2.3 %copy.48 = bf16[1,4,576,128]{3,1,0,2:T(4,128)(2,1)} copy(bf16[1,4,576,128]{3,2,1,0:T(8,128)(2,1)} %param.6) | data formatting | bytes 1179648 | tf_op args[0]
  2.4 6.3 %all-to-all-start = ((bf16[1,4,576,128]{3,1,0,2:T(4,128)(2,1)}), bf16[1,4,576,128]{3,1,0,2:T(4,128)(2,1)S(1)}, u32[]{:S(2)}, u32[]{:S(2)}) async-start(bf16[1,4,576,128]{3,1,0,2:T(4,128)(2,1)} %copy.48), calls=%async_computation | async-start | bytes 1179648 | tf_op jit(solution)/shard_map/all_to_all | solution.py:39
  9.3 15.3 %all-to-all-done = bf16[1,4,576,128]{3,1,0,2:T(4,128)(2,1)S(1)} async-done(((bf16[1,4,576,128]{3,1,0,2:T(4,128)(2,1)}), bf16[1,4,576,128]{3,1,0,2:T(4,128)(2,1)S(1)}, u32[]{:S(2)}, u32[]{:S(2)}) %all-to-all-start) | async-done | bytes 589856 | tf_op jit(solution)/shard_map/all_to_all | solution.py:39
  24.7 1.5 %fusion.40 = bf16[1,16,144,128]{3,2,0,1:T(8,128)(2,1)} fusion(f32[128]{0:T(128)S(1)} %get-tuple-element.90, bf16[1,16,144,128]{3,2,1,0:T(8,128)(2,1)S(1)} %bitcast.185, f32[128]{0:T(128)S(1)} %get-tuple-element.89, f32[128]{0:T(128)S(1)} %get-tuple-element.88, f32[128]{0:T(128)S(1)} %get-tuple-element.87, f32[128]{0:T(128)S(1)} %get-tuple-element.86, ...), kind=kLoop, calls=%fused_computation.114 | loop fusion | flops 7962624 | bytes 1184256 | tf_op jit(solution)/shard_map/convert_element_type | solution.py:15
  26.2 3.5 %all-to-all-start.1 = ((bf16[1,16,144,128]{3,2,0,1:T(8,128)(2,1)}), bf16[1,16,144,128]{3,2,0,1:T(8,128)(2,1)S(1)}, u32[]{:S(2)}, u32[]{:S(2)}) async-start(bf16[1,16,144,128]{3,2,0,1:T(8,128)(2,1)} %fusion.40), calls=%async_computation.1 | async-start | bytes 1179648 | tf_op jit(solution)/shard_map/all_to_all | solution.py:42
  31.5 13.6 %all-to-all-done.1 = bf16[1,16,144,128]{3,2,0,1:T(8,128)(2,1)S(1)} async-done(((bf16[1,16,144,128]{3,2,0,1:T(8,128)(2,1)}), bf16[1,16,144,128]{3,2,0,1:T(8,128)(2,1)S(1)}, u32[]{:S(2)}, u32[]{:S(2)}) %all-to-all-start.1) | async-done | bytes 589856 | tf_op jit(solution)/shard_map/all_to_all | solution.py:42
  48.3 0.9 fusion.52
  49.9 1.6 %multiply_reduce_fusion.1 = f32[4,4,144]{2,0,1:T(4,128)} fusion(f32[1,4,4,144,128]{4,3,1,2,0:T(8,128)S(1)} %get-tuple-element.8, f32[4,4,144]{2,0,1:T(4,128)S(1)} %broadcast_multiply_fusion.1), kind=kLoop, calls=%fused_computation.96 | loop fusion | flops 882432 | bytes 1198080 | tf_op jit(solution)/shard_map/reduce_sum | solution.py:25
  51.4 1.4 %div.65 = f32[4,576]{1,0:T(4,128)} reshape(f32[4,4,144]{2,1,0:T(4,128)} %copy.61) | data formatting | bytes 18432 | tf_op jit(solution)/shard_map/div | solution.py:23
  54.2 1.4 %sqrt.23 = f32[4,576]{1,0:T(4,128)} reshape(f32[4,4,144]{2,1,0:T(4,128)} %copy.62) | data formatting | bytes 18432 | tf_op jit(solution)/shard_map/sqrt | solution.py:26
  55.6 4.8 %multiply_convert_fusion.1 = bf16[1,4,576,128]{3,2,1,0:T(8,128)(2,1)S(1)} fusion(f32[128]{0:T(128)} %get-tuple-element.81, f32[4,576]{1,0:T(4,128)} %sqrt.23, f32[4,576]{1,0:T(4,128)} %div.65, f32[128]{0:T(128)} %get-tuple-element.60, f32[128]{0:T(128)} %get-tuple-element.61, f32[128]{0:T(128)} %get-tuple-element.62, f32[128]{0:T(128)} %get-tuple-element.63, ...), kind=kLoop, calls=%fused_computation.95 | loop fusion | flops 15925248 | bytes 5921792 | tf_op jit(solution)/shard_map/convert_element_type | solution.py:26
  60.4 5.4 %fusion.2 = bf16[2304,256]{1,0:T(8,128)(2,1)S(1)} fusion(bf16[2304,128]{1,0:T(8,128)(2,1)S(1)} %bitcast.190, bf16[2,128,256]{2,1,0:T(8,128)(2,1)S(1)} %copy-done.60), kind=kOutput, calls=%fused_computation.4 | convolution fusion | flops 189333504 | bytes 1835008 | tf_op jit(solution)/shard_map/dot_general | solution.py:29
  66.8 17.8 %all_to_all.72 = bf16[1,4,576,128]{3,1,0,2:T(4,128)(2,1)S(1)} all-to-all(bf16[1,4,576,128]{3,1,0,2:T(4,128)(2,1)S(1)} %copy.63), channel_id=1, replica_groups=mesh['section'=4,'band'=4,'members'=2] {'band'}, dimensions={2} | all-to-all | bytes 1179648 | tf_op jit(solution)/shard_map/all_to_all | solution.py:39
  85.3 1.5 %fusion.41 = bf16[1,16,144,128]{3,2,0,1:T(8,128)(2,1)} fusion(f32[128]{0:T(128)S(1)} %copy-done.51, bf16[1,16,144,128]{3,2,1,0:T(8,128)(2,1)S(1)} %bitcast.184, f32[128]{0:T(128)S(1)} %copy-done.52, f32[128]{0:T(128)S(1)} %copy-done.53, f32[128]{0:T(128)S(1)} %copy-done.54, f32[128]{0:T(128)S(1)} %copy-done.55, f32[128]{0:T(128)S(1)} %copy-done.56, ...), kind=kLoop, calls=%fused_computation.115 | loop fusion | flops 7962624 | bytes 1184256 | tf_op jit(solution)/shard_map/convert_element_type | solution.py:15
  86.8 3.7 %all-to-all-start.3 = ((bf16[1,16,144,128]{3,2,0,1:T(8,128)(2,1)}), bf16[1,16,144,128]{3,2,0,1:T(8,128)(2,1)S(1)}, u32[]{:S(2)}, u32[]{:S(2)}) async-start(bf16[1,16,144,128]{3,2,0,1:T(8,128)(2,1)} %fusion.41), calls=%async_computation.3 | async-start | bytes 1179648 | tf_op jit(solution)/shard_map/all_to_all | solution.py:42
  91.1 14.3 %all-to-all-done.3 = bf16[1,16,144,128]{3,2,0,1:T(8,128)(2,1)S(1)} async-done(((bf16[1,16,144,128]{3,2,0,1:T(8,128)(2,1)}), bf16[1,16,144,128]{3,2,0,1:T(8,128)(2,1)S(1)}, u32[]{:S(2)}, u32[]{:S(2)}) %all-to-all-start.3) | async-done | bytes 589856 | tf_op jit(solution)/shard_map/all_to_all | solution.py:42
  108.5 0.9 copy-done.1
  109.5 0.9 fusion.50
  111.0 1.6 %multiply_reduce_fusion = f32[4,4,144]{2,0,1:T(4,128)} fusion(f32[1,4,4,144,128]{4,3,1,2,0:T(8,128)S(1)} %get-tuple-element.6, f32[4,4,144]{2,0,1:T(4,128)S(1)} %broadcast_multiply_fusion), kind=kLoop, calls=%fused_computation.93 | loop fusion | flops 882432 | bytes 1198080 | tf_op jit(solution)/shard_map/reduce_sum | solution.py:25
  112.6 1.4 %div.70 = f32[4,576]{1,0:T(4,128)} reshape(f32[4,4,144]{2,1,0:T(4,128)} %copy.76) | data formatting | bytes 18432 | tf_op jit(solution)/shard_map/div | solution.py:23
  115.3 1.4 %sqrt.25 = f32[4,576]{1,0:T(4,128)} reshape(f32[4,4,144]{2,1,0:T(4,128)} %copy.77) | data formatting | bytes 18432 | tf_op jit(solution)/shard_map/sqrt | solution.py:26
  116.7 4.9 %multiply_convert_fusion = bf16[1,4,576,128]{3,2,1,0:T(8,128)(2,1)S(1)} fusion(f32[128]{0:T(128)} %get-tuple-element.82, f32[4,576]{1,0:T(4,128)} %sqrt.25, f32[4,576]{1,0:T(4,128)} %div.70, f32[128]{0:T(128)} %get-tuple-element.42, f32[128]{0:T(128)} %get-tuple-element.43, f32[128]{0:T(128)} %get-tuple-element.44, f32[128]{0:T(128)} %get-tuple-element.45, ...), kind=kLoop, calls=%fused_computation.92 | loop fusion | flops 15925248 | bytes 5921792 | tf_op jit(solution)/shard_map/convert_element_type | solution.py:26
  121.7 5.4 %fusion.5 = bf16[2304,256]{1,0:T(8,128)(2,1)S(1)} fusion(bf16[2304,128]{1,0:T(8,128)(2,1)S(1)} %bitcast.191, bf16[2,128,256]{2,1,0:T(8,128)(2,1)S(1)} %copy-done.61), kind=kOutput, calls=%fused_computation.7 | convolution fusion | flops 189333504 | bytes 1835008 | tf_op jit(solution)/shard_map/dot_general | solution.py:29
  127.1 1.3 %fusion.22 = bf16[1,4,576,128]{3,2,1,0:T(8,128)(2,1)} fusion(bf16[4,576,256]{2,1,0:T(8,128)(2,1)S(1)} %bitcast.188, bf16[1,4,576,128]{3,2,1,0:T(8,128)(2,1)S(1)} %fusion.23, bf16[2,256,128]{2,1,0:T(8,128)(2,1)S(1)} %copy-done.19), kind=kOutput, calls=%fused_computation.42 | convolution fusion | flops 151879680 | bytes 2424832 | tf_op jit(solution)/shard_map/dot_general | solution.py:31
  (177 shorter events, 14.4 us)
Async XLA Ops:
  0.0 8.7 %copy-start.29 = (bf16[2,9,128]{2,0,1:T(2,128)(2,1)S(1)}, bf16[2,9,128]{2,0,1:T(2,128)(2,1)}, u32[]{:S(2)}) copy-start(bf16[2,9,128]{2,0,1:T(2,128)(2,1)} %param.7) | copy-start | bytes 13828
  2.4 22.2 %all-to-all-start = ((bf16[1,4,576,128]{3,1,0,2:T(4,128)(2,1)}), bf16[1,4,576,128]{3,1,0,2:T(4,128)(2,1)S(1)}, u32[]{:S(2)}, u32[]{:S(2)}) async-start(bf16[1,4,576,128]{3,1,0,2:T(4,128)(2,1)} %copy.48), calls=%async_computation | async-start | bytes 1179648 | tf_op jit(solution)/shard_map/all_to_all | solution.py:39
  24.7 5.0 %copy-start.59 = (f32[2,128]{1,0:T(2,128)S(1)}, f32[2,128]{1,0:T(2,128)}, u32[]{:S(2)}) copy-start(f32[2,128]{1,0:T(2,128)} %param.9) | copy-start | bytes 3076
  24.7 5.6 %copy-start.30 = (bf16[2,9,128]{2,0,1:T(2,128)(2,1)S(1)}, bf16[2,9,128]{2,0,1:T(2,128)(2,1)}, u32[]{:S(2)}) copy-start(bf16[2,9,128]{2,0,1:T(2,128)(2,1)} %param.8) | copy-start | bytes 13828
  26.2 18.9 %all-to-all-start.1 = ((bf16[1,16,144,128]{3,2,0,1:T(8,128)(2,1)}), bf16[1,16,144,128]{3,2,0,1:T(8,128)(2,1)S(1)}, u32[]{:S(2)}, u32[]{:S(2)}) async-start(bf16[1,16,144,128]{3,2,0,1:T(8,128)(2,1)} %fusion.40), calls=%async_computation.1 | async-start | bytes 1179648 | tf_op jit(solution)/shard_map/all_to_all | solution.py:42
  45.1 2.1 %copy-start.27 = (bf16[1,4,3,128]{3,2,1,0:T(4,128)(2,1)}, bf16[1,4,3,128]{3,2,1,0:T(4,128)(2,1)S(1)}, u32[]{:S(2)}) copy-start(bf16[1,4,3,128]{3,2,1,0:T(4,128)(2,1)S(1)} %get-tuple-element.37) | copy-start | bytes 9220
  45.1 2.2 %copy-start.28 = (bf16[1,4,3,128]{3,2,1,0:T(4,128)(2,1)}, bf16[1,4,3,128]{3,2,1,0:T(4,128)(2,1)S(1)}, u32[]{:S(2)}) copy-start(bf16[1,4,3,128]{3,2,1,0:T(4,128)(2,1)S(1)} %get-tuple-element.38) | copy-start | bytes 9220
  45.2 2.3 %copy-start.22 = (bf16[1,4,6,128]{3,2,1,0:T(8,128)(2,1)}, bf16[1,4,6,128]{3,2,1,0:T(8,128)(2,1)S(1)}, u32[]{:S(2)}) copy-start(bf16[1,4,6,128]{3,2,1,0:T(8,128)(2,1)S(1)} %get-tuple-element.33) | copy-start | bytes 18436
  45.2 2.5 %copy-start.24 = (bf16[1,4,6,128]{3,2,1,0:T(8,128)(2,1)}, bf16[1,4,6,128]{3,2,1,0:T(8,128)(2,1)S(1)}, u32[]{:S(2)}) copy-start(bf16[1,4,6,128]{3,2,1,0:T(8,128)(2,1)S(1)} %get-tuple-element.34) | copy-start | bytes 18436
  49.2 6.4 %copy-start.5 = (bf16[1,4,567,128]{3,2,1,0:T(8,128)(2,1)S(1)}, bf16[1,4,567,128]{3,2,1,0:T(8,128)(2,1)}, u32[]{:S(2)}) copy-start(bf16[1,4,567,128]{3,2,1,0:T(8,128)(2,1)} %copy-done.4) | copy-start | bytes 1741828
  49.2 6.4 %copy-start.23 = (bf16[1,4,6,128]{3,2,1,0:T(8,128)(2,1)S(1)}, bf16[1,4,6,128]{3,2,1,0:T(8,128)(2,1)}, u32[]{:S(2)}) copy-start(bf16[1,4,6,128]{3,2,1,0:T(8,128)(2,1)} %copy-done.22) | copy-start | bytes 18436
  55.6 4.8 %copy-start.60 = (bf16[2,128,256]{2,1,0:T(8,128)(2,1)S(1)}, bf16[2,128,256]{2,1,0:T(8,128)(2,1)}, u32[]{:S(2)}) copy-start(bf16[2,128,256]{2,1,0:T(8,128)(2,1)} %param.10) | copy-start | bytes 393220
  60.4 5.5 %copy-start.11 = (bf16[1,4,576,128]{3,2,1,0:T(8,128)(2,1)S(1)}, bf16[1,4,576,128]{3,2,1,0:T(8,128)(2,1)}, u32[]{:S(2)}) copy-start(bf16[1,4,576,128]{3,2,1,0:T(8,128)(2,1)} %param.6) | copy-start | bytes 1769476
  60.4 5.5 %copy-start.18 = (bf16[2,256,128]{2,1,0:T(8,128)(2,1)S(1)}, bf16[2,256,128]{2,1,0:T(8,128)(2,1)}, u32[]{:S(2)}) copy-start(bf16[2,256,128]{2,1,0:T(8,128)(2,1)} %param.11) | copy-start | bytes 393220
  85.3 5.2 %copy-start.31 = (f32[1,9,128]{2,0,1:T(1,128)S(1)}, f32[1,9,128]{2,0,1:T(1,128)}, u32[]{:S(2)}) copy-start(f32[1,9,128]{2,0,1:T(1,128)} %get-tuple-element.80) | copy-start | bytes 13828
  86.8 18.6 %all-to-all-start.3 = ((bf16[1,16,144,128]{3,2,0,1:T(8,128)(2,1)}), bf16[1,16,144,128]{3,2,0,1:T(8,128)(2,1)S(1)}, u32[]{:S(2)}, u32[]{:S(2)}) async-start(bf16[1,16,144,128]{3,2,0,1:T(8,128)(2,1)} %fusion.41), calls=%async_computation.3 | async-start | bytes 1179648 | tf_op jit(solution)/shard_map/all_to_all | solution.py:42
  105.4 2.5 %copy-start.25 = (bf16[1,4,3,128]{3,2,1,0:T(4,128)(2,1)}, bf16[1,4,3,128]{3,2,1,0:T(4,128)(2,1)S(1)}, u32[]{:S(2)}) copy-start(bf16[1,4,3,128]{3,2,1,0:T(4,128)(2,1)S(1)} %get-tuple-element.21) | copy-start | bytes 9220
  105.4 2.7 %copy-start.26 = (bf16[1,4,3,128]{3,2,1,0:T(4,128)(2,1)}, bf16[1,4,3,128]{3,2,1,0:T(4,128)(2,1)S(1)}, u32[]{:S(2)}) copy-start(bf16[1,4,3,128]{3,2,1,0:T(4,128)(2,1)S(1)} %get-tuple-element.22) | copy-start | bytes 9220
  105.5 2.7 %copy-start.20 = (bf16[1,4,6,128]{3,2,1,0:T(8,128)(2,1)}, bf16[1,4,6,128]{3,2,1,0:T(8,128)(2,1)S(1)}, u32[]{:S(2)}) copy-start(bf16[1,4,6,128]{3,2,1,0:T(8,128)(2,1)S(1)} %get-tuple-element.17) | copy-start | bytes 18436
  105.5 3.0 %copy-start.21 = (bf16[1,4,6,128]{3,2,1,0:T(8,128)(2,1)}, bf16[1,4,6,128]{3,2,1,0:T(8,128)(2,1)S(1)}, u32[]{:S(2)}) copy-start(bf16[1,4,6,128]{3,2,1,0:T(8,128)(2,1)S(1)} %get-tuple-element.18) | copy-start | bytes 18436
  105.5 2.4 %copy-start.12 = (bf16[1,4,9,128]{3,2,1,0:T(8,128)(2,1)}, bf16[1,4,9,128]{3,2,1,0:T(8,128)(2,1)S(1)}, u32[]{:S(2)}) copy-start(bf16[1,4,9,128]{3,2,1,0:T(8,128)(2,1)S(1)} %get-tuple-element.14) | copy-start | bytes 27652
  105.5 2.0 %copy-start.15 = (bf16[1,4,12,128]{3,2,1,0:T(8,128)(2,1)}, bf16[1,4,12,128]{3,2,1,0:T(8,128)(2,1)S(1)}, u32[]{:S(2)}) copy-start(bf16[1,4,12,128]{3,2,1,0:T(8,128)(2,1)S(1)} %get-tuple-element.10) | copy-start | bytes 36868
  116.7 4.9 %copy-start.61 = (bf16[2,128,256]{2,1,0:T(8,128)(2,1)S(1)}, bf16[2,128,256]{2,1,0:T(8,128)(2,1)}, u32[]{:S(2)}) copy-start(bf16[2,128,256]{2,1,0:T(8,128)(2,1)} %param.10) | copy-start | bytes 393220
  121.7 5.5 %copy-start.19 = (bf16[2,256,128]{2,1,0:T(8,128)(2,1)S(1)}, bf16[2,256,128]{2,1,0:T(8,128)(2,1)}, u32[]{:S(2)}) copy-start(bf16[2,256,128]{2,1,0:T(8,128)(2,1)} %param.11) | copy-start | bytes 393220
  (41 other events, 39.6 us)
where the time goes:
time: 129 us; the launch traced here: 128 us
  waiting for transfers between devices  43.1 us (33%)
  other arithmetic  21.3 us (17%)
  local copies, waits for them, and re-layouts  19.1 us (15%)
  blocking collectives  17.8 us (14%)
  starting transfers between devices  13.5 us (10%)
  matrix products  12.6 us (10%)
    all_to_all x2, waiting for transfers between devices, shards(): lax.all_to_all(mixed, 'band', split_axis=1, concat_axis=2, tiled=True)  27.8 us
    all_to_all x1, blocking collectives, shards(): lax.all_to_all(state, 'band', split_axis=2, concat_axis=1, tiled=True)  17.8 us
    all_to_all x1, waiting for transfers between devices, shards(): lax.all_to_all(state, 'band', split_axis=2, concat_axis=1, tiled=True)  15.3 us
    dot_general x2, matrix products, layer_rest(): jnp.dot(flat, proj_in, preferred_element_type=jnp.float32)  10.9 us
    convert_element_type x2, other arithmetic, layer_rest(): normed = (centred / jnp.sqrt(var + 1e-06) * gain).astype(jnp.bfloat16)  9.7 us
    all_to_all x2, starting transfers between devices, shards(): lax.all_to_all(mixed, 'band', split_axis=1, concat_axis=2, tiled=True)  7.14 us
    all_to_all x1, starting transfers between devices, shards(): lax.all_to_all(state, 'band', split_axis=2, concat_axis=1, tiled=True)  6.32 us
    unnamed x125, local copies, waits for them, and re-layouts  5.9 us
  transfers between devices with their start and end apart: 3, of which 3 were waited for; matrix products, arithmetic and copies ran while one was open for 2% of the time, Pallas kernels for 0%

commit v1 on v0

v1 whole, which is shorter than its diff:
```python
import functools

import jax
import jax.numpy as jnp
from jax import lax
from jax.experimental import pallas as pl
from jax.experimental.pallas import tpu as pltpu
from jax.sharding import PartitionSpec as P

DLON = 3
LAYERS = 2
TAPS = 9
REACH = TAPS // 2
PAD = 16
CHUNKS = 1
TILE = 32


def gelu(x):
    return 0.5 * x * (1.0 + lax.erf(x * 0.7071067811865476))


def chunk_kernel(first, last, width, *refs):
    refs = list(refs)
    lat_w, lon_w, gain, w_in, w_out, own, above, below = refs[:8]
    refs = refs[8:]
    if not first:
        prev_own, prev_mix = refs[:2]
        refs = refs[2:]
    if last and not first:
        first_own, first_mix = refs[:2]
        refs = refs[2:]
    out = refs.pop(0)
    if not last:
        tail = refs.pop(0)
    if first and not last:
        head = refs.pop(0)
    mix, state = refs
    rows = own.shape[0]
    channels = own.shape[2]
    start = 0 if first else 2 * PAD

    if not first:
        mix[:, : 2 * PAD] = prev_mix[...].astype(jnp.float32)
        state[:, : 2 * PAD] = prev_own[:, prev_own.shape[1] - 2 * PAD :]
    if last and not first:
        mix[:, start + width :] = first_mix[...].astype(jnp.float32)
        state[:, start + width :] = first_own[:, : 2 * PAD]

    lat_tap = [jnp.broadcast_to(lat_w[k : k + 1], (PAD, channels)) for k in range(TAPS)]

    def mix_tile(t, carry):
        at = pl.multiple_of(t * PAD, PAD)
        to = pl.multiple_of(start + t * PAD, PAD)
        strip = [above[r, pl.ds(at, PAD)] for r in range(REACH)]
        mine = [own[r, pl.ds(at, PAD)] for r in range(rows)]
        strip = strip + mine + [below[r, pl.ds(at, PAD)] for r in range(REACH)]
        strip = [s.astype(jnp.float32) for s in strip]
        for r in range(rows):
            total = strip[r] * lat_tap[0]
            for k in range(1, TAPS):
                total = total + strip[r + k] * lat_tap[k]
            mix[r, pl.ds(to, PAD)] = total.astype(jnp.bfloat16).astype(jnp.float32)
            state[r, pl.ds(to, PAD)] = mine[r]
        return carry

    lax.fori_loop(0, width // PAD, mix_tile, 0)

    if not last:
        tail[...] = mix[:, start + width - 2 * PAD : start + width].astype(jnp.bfloat16)
    if first and not last:
        head[...] = mix[:, : 2 * PAD].astype(jnp.bfloat16)
    if first and last:
        mix[:, width:] = mix[:, : 2 * PAD]
        state[:, width:] = state[:, : 2 * PAD]

    lon_tap = [lon_w[k : k + 1] for k in range(TAPS)]
    scale = gain[...]
    made = out.shape[1]

    def rest(at, tile):
        parts = []
        for r in range(rows):
            lon = mix[r, pl.ds(at + PAD - DLON * REACH, tile)] * lon_tap[0]
            for k in range(1, TAPS):
                lon = lon + mix[r, pl.ds(at + PAD + DLON * (k - REACH), tile)] * lon_tap[k]
            parts.append(lon)
        lon = jnp.concatenate(parts, axis=0)
        mean = jnp.mean(lon, axis=-1, keepdims=True)
        centred = lon - mean
        var = jnp.mean(centred * centred, axis=-1, keepdims=True)
        normed = (centred * lax.rsqrt(var + 1e-06) * scale).astype(jnp.bfloat16)
        hidden = jnp.dot(normed, w_in[...], preferred_element_type=jnp.float32)
        hidden = gelu(hidden).astype(jnp.bfloat16)
        delta = jnp.dot(hidden, w_out[...], preferred_element_type=jnp.float32)
        for r in range(rows):
            new = state[r, pl.ds(at + PAD, tile)].astype(jnp.float32) + delta[r * tile : (r + 1) * tile]
            out[r, pl.ds(at, tile)] = new.astype(jnp.bfloat16)

    for at in range(0, made, TILE):
        rest(at, min(TILE, made - at))


def layer_chunk(weights, chunk, prev, first_chunk, first, last):
    own, above, below = chunk
    rows, width, channels = own.shape
    made = width + (0 if first else PAD) + (0 if last else -PAD) + (PAD if last else 0) - (PAD if first else 0)
    window = made + 2 * PAD
    args = list(weights) + [own, above, below]
    if not first:
        args += list(prev)
    if last and not first:
        args += list(first_chunk)
    strip = jax.ShapeDtypeStruct((rows, 2 * PAD, channels), jnp.bfloat16)
    outs = [jax.ShapeDtypeStruct((rows, made, channels), jnp.bfloat16)]
    if not last:
        outs.append(strip)
    if first and not last:
        outs.append(strip)
    cells = rows * made
    hidden = weights[3].shape[1]
    return pl.pallas_call(
        functools.partial(chunk_kernel, first, last, width),
        out_shape=outs,
        in_specs=[pl.BlockSpec(memory_space=pltpu.VMEM)] * len(args),
        out_specs=[pl.BlockSpec(memory_space=pltpu.VMEM)] * len(outs),
        scratch_shapes=[
            pltpu.VMEM((rows, window, channels), jnp.float32),
            pltpu.VMEM((rows, window, channels), jnp.bfloat16),
        ],
        compiler_params=pltpu.CompilerParams(vmem_limit_bytes=24 * 2**20),
        cost_estimate=pl.CostEstimate(
            flops=4 * cells * channels * hidden, bytes_accessed=8 * cells * channels, transcendentals=cells * hidden
        ),
    )(*args)


def splits(total):
    tiles = total // PAD
    edges = [PAD * ((tiles * c) // CHUNKS) for c in range(CHUNKS)] + [total]
    return [(lo, hi) for lo, hi in zip(edges[:-1], edges[1:])]


def member_step(state, weights, bands):
    rows, lons, _ = state.shape
    up = [(b, b + 1) for b in range(bands - 1)]
    down = [(b + 1, b) for b in range(bands - 1)]
    chunks = [state[:, lo:hi] for lo, hi in splits(lons)]
    for layer in range(LAYERS):
        halos = [
            (lax.ppermute(own[rows - REACH :], "band", up), lax.ppermute(own[:REACH], "band", down))
            for own in chunks
        ]
        made, prev, first_chunk = [], None, None
        for c, own in enumerate(chunks):
            first, last = c == 0, c == len(chunks) - 1
            got = layer_chunk(weights[layer], (own,) + halos[c], prev, first_chunk, first, last)
            made.append(got[0])
            if not last:
                prev = (own, got[1])
            if first and not last:
                first_chunk = (own[:, : 2 * PAD], got[2])
        chunks = made
    whole = jnp.concatenate(chunks, axis=1)
    return jnp.roll(whole, LAYERS * PAD, axis=1)


def solution(mesh):
    bands = mesh.shape["band"]

    def shards(fields, lat_taps, lon_taps, gains, w_in, w_out):
        weights = [
            (
                lat_taps[layer].astype(jnp.float32),
                lon_taps[layer].astype(jnp.float32),
                gains[layer : layer + 1],
                w_in[layer],
                w_out[layer],
            )
            for layer in range(LAYERS)
        ]
        return jnp.stack([member_step(fields[m], weights, bands) for m in range(fields.shape[0])])

    return jax.shard_map(
        shards,
        mesh=mesh,
        in_specs=(P(("members", "section"), "band", None, None), P(), P(), P(), P(), P()),
        out_specs=P(("members", "section"), "band", None, None),
        check_vma=False,
    )
```

time: 129 us -> 45.2 us (0.35)
  waiting for transfers between devices: 43.1 us -> 20.4 us
  other arithmetic: 21.3 us -> 0.86 us
  blocking collectives: 17.8 us -> 0 us
  local copies, waits for them, and re-layouts: 19.1 us -> 4.12 us
  matrix products: 12.6 us -> 0 us
  Pallas kernels: 0 us -> 6.09 us
    all_to_all x3 -> x0, waiting for transfers between devices: 43.1 us -> none  [the longest x2 27.8 us: shards(): lax.all_to_all(mixed, 'band', split_axis=1, concat_axis=2, tiled=True)]
    ppermute x0 -> x4, waiting for transfers between devices: none -> 20.4 us  [the longest x2 17.9 us: member_step(): lax.ppermute(own[:REACH], 'band', down)]
    all_to_all x1 -> x0, blocking collectives: 17.8 us -> none  [shards(): lax.all_to_all(state, 'band', split_axis=2, concat_axis=1, tiled=True)]
    convert_element_type x22 -> x2, other arithmetic: 14.9 us -> 0.01 us  [shards(): lon_taps[layer].astype(jnp.float32)]
    all_to_all x3 -> x0, starting transfers between devices: 13.5 us -> none  [the longest x2 7.14 us: shards(): lax.all_to_all(mixed, 'band', split_axis=1, concat_axis=2, tiled=True)]
    ppermute x0 -> x4, starting transfers between devices: none -> 13.2 us  [the longest x2 10.5 us: member_step(): lax.ppermute(own[rows - REACH:], 'band', up)]
    dot_general x4 -> x0, matrix products: 12.6 us -> none  [the longest x2 10.9 us: layer_rest(): jnp.dot(flat, proj_in, preferred_element_type=jnp.float32)]
    pallas_call x0 -> x2, Pallas kernels: none -> 6.09 us  [layer_chunk(): pl.pallas_call(functools.partial(chunk_kernel, first, last, width), out_s...]
  transfers between devices with their start and end apart: 3 -> 4, of which waited for: 3 -> 4; matrix products, arithmetic and copies ran while one was open for 2% -> 9% of each run, Pallas kernels for 0% -> 0%
where the time goes in v1:
time: 45.2 us; the launch traced here: 44.8 us
  waiting for transfers between devices  20.4 us (45%)
  starting transfers between devices  13.2 us (29%)
  Pallas kernels  6.09 us (13%)
  local copies, waits for them, and re-layouts  4.12 us (9%)
  other arithmetic  0.86 us (2%)
    ppermute x2, waiting for transfers between devices, member_step(): lax.ppermute(own[:REACH], 'band', down)  17.9 us
    ppermute x2, starting transfers between devices, member_step(): lax.ppermute(own[rows - REACH:], 'band', up)  10.5 us
    pallas_call x2, Pallas kernels, layer_chunk(): pl.pallas_call(functools.partial(chunk_kernel, first, last, width), out_s...  6.09 us
    ppermute x2, starting transfers between devices, member_step(): lax.ppermute(own[:REACH], 'band', down)  2.7 us
    ppermute x2, waiting for transfers between devices, member_step(): lax.ppermute(own[rows - REACH:], 'band', up)  2.47 us
  transfers between devices with their start and end apart: 4, of which 4 were waited for; matrix products, arithmetic and copies ran while one was open for 9% of the time, Pallas kernels for 0%

profile of v1, /device:TPU:0, one launch (start us, length us, event | category | flops | bytes accessed | tf_op | source)
XLA Modules:
  0.0 44.8 jit_solution(4466137942314509397)
XLA Ops:
  0.0 0.0 copy-start
  0.0 1.4 %collective-permute-start.1 = (bf16[4,576,128]{2,1,0:T(8,128)(2,1)}, bf16[4,576,128]{2,1,0:T(8,128)(2,1)S(1)}, u32[]{:S(2)}, u32[]{:S(2)}) collective-permute-start(bf16[4,576,128]{2,1,0:T(8,128)(2,1)} %bitcast.31), channel_id=1, source_target_pairs={{2,0},{4,2},{6,4},{3,1},{5,3},{7,5},{10,8},{12,10},{14,12},{11,9},... | collective-permute-start | bytes 1769480 | tf_op jit(solution)/shard_map/ppermute | solution.py:151
  1.4 5.6 %collective-permute-start = (bf16[4,576,128]{2,1,0:T(8,128)(2,1)}, bf16[4,576,128]{2,1,0:T(8,128)(2,1)S(1)}, u32[]{:S(2)}, u32[]{:S(2)}) collective-permute-start(bf16[4,576,128]{2,1,0:T(8,128)(2,1)} %bitcast.32), channel_id=1, source_target_pairs={{0,2},{2,4},{4,6},{1,3},{3,5},{5,7},{8,10},{10,12},{12,14},{9,11},... | collective-permute-start | bytes 1769480 | tf_op jit(solution)/shard_map/ppermute | solution.py:151
  7.0 0.8 %fusion.5 = (bf16[1,9,128]{2,0,1:T(2,128)(2,1)S(1)}, bf16[1,9,128]{2,0,1:T(2,128)(2,1)S(1)}) fusion(bf16[2,9,128]{2,0,1:T(2,128)(2,1)} %param.7), kind=kLoop, calls=%fused_computation.14 | loop fusion | bytes 9216 | tf_op jit(solution)/shard_map/slice | solution.py:174
  7.8 0.8 %fusion.4 = (bf16[1,9,128]{2,0,1:T(2,128)(2,1)S(1)}, bf16[1,9,128]{2,0,1:T(2,128)(2,1)S(1)}) fusion(bf16[2,9,128]{2,0,1:T(2,128)(2,1)} %param.8), kind=kLoop, calls=%fused_computation.13 | loop fusion | bytes 9216 | tf_op jit(solution)/shard_map/slice | solution.py:175
  8.6 0.8 %fusion.6 = (f32[1,128]{1,0:T(1,128)S(1)}, f32[1,128]{1,0:T(1,128)S(1)}) fusion(f32[2,128]{1,0:T(2,128)} %param.9), kind=kLoop, calls=%fused_computation.15 | loop fusion | bytes 2048 | tf_op jit(solution)/shard_map/slice | solution.py:176
  9.4 0.9 %slice_bitcast_fusion.1 = (bf16[128,256]{1,0:T(8,128)(2,1)S(1)}, bf16[128,256]{1,0:T(8,128)(2,1)S(1)}) fusion(bf16[2,128,256]{2,1,0:T(8,128)(2,1)} %param.10), kind=kLoop, calls=%fused_computation.2 | loop fusion | bytes 262144 | tf_op jit(solution)/shard_map/squeeze | solution.py:177
  10.2 0.9 %slice_bitcast_fusion = (bf16[256,128]{1,0:T(8,128)(2,1)S(1)}, bf16[256,128]{1,0:T(8,128)(2,1)S(1)}) fusion(bf16[2,256,128]{2,1,0:T(8,128)(2,1)} %param.11), kind=kLoop, calls=%fused_computation.1 | loop fusion | bytes 262144 | tf_op jit(solution)/shard_map/squeeze | solution.py:178
  11.1 7.5 %collective-permute-done.1.refs_7_ = bf16[4,576,128]{2,1,0:T(8,128)(2,1)S(1)} collective-permute-done((bf16[4,576,128]{2,1,0:T(8,128)(2,1)}, bf16[4,576,128]{2,1,0:T(8,128)(2,1)S(1)}, u32[]{:S(2)}, u32[]{:S(2)}) %collective-permute-start.1) | collective-permute-done | bytes 589856 | tf_op jit(solution)/shard_map/ppermute | solution.py:151
  18.6 1.3 %collective-permute-done.refs_6_ = bf16[4,576,128]{2,1,0:T(8,128)(2,1)S(1)} collective-permute-done((bf16[4,576,128]{2,1,0:T(8,128)(2,1)}, bf16[4,576,128]{2,1,0:T(8,128)(2,1)S(1)}, u32[]{:S(2)}, u32[]{:S(2)}) %collective-permute-start) | collective-permute-done | bytes 589856 | tf_op jit(solution)/shard_map/ppermute | solution.py:151
  19.9 0.0 copy-done
  19.9 3.0 %shard_map.64.refs_5_ = bf16[4,576,128]{2,1,0:T(8,128)(2,1)S(1)} custom-call(f32[9,128]{1,0:T(8,128)S(1)} %get-tuple-element.16.refs_0_, f32[9,128]{1,0:T(8,128)S(1)} %get-tuple-element.15.refs_1_, f32[1,128]{1,0:T(1,128)S(1)} %get-tuple-element.13.refs_2_, bf16[128,256]{1,0:T(8,128)(2,1)S(1)} %get-tuple-element.7.refs_3_, ...), custom_call_target="tpu_custom_call" | custom-call | flops 301989888 | bytes 2359296 | tf_op jit(solution)/shard_map/pallas_call | solution.py:122
  22.9 1.3 %collective-permute-start.3 = (bf16[4,576,128]{2,1,0:T(8,128)(2,1)S(1)}, bf16[4,576,128]{2,1,0:T(8,128)(2,1)S(1)}, u32[]{:S(2)}, u32[]{:S(2)}) collective-permute-start(bf16[4,576,128]{2,1,0:T(8,128)(2,1)S(1)} %shard_map.64.refs_5_), channel_id=1, source_target_pairs={{2,0},{4,2},{6,4},{3,1},{5,3},{7,5},{10,8},{12,10},{14,12},{11,9},... | collective-permute-start | bytes 1769480 | tf_op jit(solution)/shard_map/ppermute | solution.py:151
  24.2 4.9 %collective-permute-start.2 = (bf16[4,576,128]{2,1,0:T(8,128)(2,1)S(1)}, bf16[4,576,128]{2,1,0:T(8,128)(2,1)S(1)}, u32[]{:S(2)}, u32[]{:S(2)}) collective-permute-start(bf16[4,576,128]{2,1,0:T(8,128)(2,1)S(1)} %shard_map.64.refs_5_), channel_id=1, source_target_pairs={{0,2},{2,4},{4,6},{1,3},{3,5},{5,7},{8,10},{10,12},{12,14},{9,11},... | collective-permute-start | bytes 1769480 | tf_op jit(solution)/shard_map/ppermute | solution.py:151
  29.2 10.5 %collective-permute-done.3.refs_7_ = bf16[4,576,128]{2,1,0:T(8,128)(2,1)S(1)} collective-permute-done((bf16[4,576,128]{2,1,0:T(8,128)(2,1)S(1)}, bf16[4,576,128]{2,1,0:T(8,128)(2,1)S(1)}, u32[]{:S(2)}, u32[]{:S(2)}) %collective-permute-start.3) | collective-permute-done | bytes 589856 | tf_op jit(solution)/shard_map/ppermute | solution.py:151
  39.7 1.2 %collective-permute-done.2.refs_6_ = bf16[4,576,128]{2,1,0:T(8,128)(2,1)S(1)} collective-permute-done((bf16[4,576,128]{2,1,0:T(8,128)(2,1)S(1)}, bf16[4,576,128]{2,1,0:T(8,128)(2,1)S(1)}, u32[]{:S(2)}, u32[]{:S(2)}) %collective-permute-start.2) | collective-permute-done | bytes 589856 | tf_op jit(solution)/shard_map/ppermute | solution.py:151
  40.8 3.0 %shard_map.65 = bf16[4,576,128]{2,1,0:T(8,128)(2,1)S(1)} custom-call(f32[9,128]{1,0:T(8,128)S(1)} %get-tuple-element.18.refs_0_, f32[9,128]{1,0:T(8,128)S(1)} %get-tuple-element.17.refs_1_, f32[1,128]{1,0:T(1,128)S(1)} %get-tuple-element.14.refs_2_, bf16[128,256]{1,0:T(8,128)(2,1)S(1)} %get-tuple-element.8.refs_3_, ...), custom_call_target="tpu_custom_call" | custom-call | flops 301989888 | bytes 2359296 | tf_op jit(solution)/shard_map/pallas_call | solution.py:122
  43.9 0.9 %maximum_bitcast_fusion = bf16[1,4,576,128]{3,2,1,0:T(8,128)(2,1)} fusion(bf16[4,544,128]{2,1,0:T(8,128)(2,1)S(1)} %slice.51, bf16[4,32,128]{2,1,0:T(8,128)(2,1)S(1)} %slice.50), kind=kLoop, calls=%fused_computation | loop fusion | flops 1179648 | bytes 1179648 | tf_op jit(solution)/shard_map/stack | solution.py:182
  (4 shorter events, 0.1 us)
Async XLA Ops:
  0.0 19.9 %copy-start = (bf16[1,4,576,128]{3,2,1,0:T(8,128)(2,1)S(1)}, bf16[1,4,576,128]{3,2,1,0:T(8,128)(2,1)}, u32[]{:S(2)}) copy-start(bf16[1,4,576,128]{3,2,1,0:T(8,128)(2,1)} %param.6) | copy-start | bytes 1769476
  0.0 18.6 %collective-permute-start.1 = (bf16[4,576,128]{2,1,0:T(8,128)(2,1)}, bf16[4,576,128]{2,1,0:T(8,128)(2,1)S(1)}, u32[]{:S(2)}, u32[]{:S(2)}) collective-permute-start(bf16[4,576,128]{2,1,0:T(8,128)(2,1)} %bitcast.31), channel_id=1, source_target_pairs={{2,0},{4,2},{6,4},{3,1},{5,3},{7,5},{10,8},{12,10},{14,12},{11,9},... | collective-permute-start | bytes 1769480 | tf_op jit(solution)/shard_map/ppermute | solution.py:151
  1.4 18.4 %collective-permute-start = (bf16[4,576,128]{2,1,0:T(8,128)(2,1)}, bf16[4,576,128]{2,1,0:T(8,128)(2,1)S(1)}, u32[]{:S(2)}, u32[]{:S(2)}) collective-permute-start(bf16[4,576,128]{2,1,0:T(8,128)(2,1)} %bitcast.32), channel_id=1, source_target_pairs={{0,2},{2,4},{4,6},{1,3},{3,5},{5,7},{8,10},{10,12},{12,14},{9,11},... | collective-permute-start | bytes 1769480 | tf_op jit(solution)/shard_map/ppermute | solution.py:151
  22.9 16.7 %collective-permute-start.3 = (bf16[4,576,128]{2,1,0:T(8,128)(2,1)S(1)}, bf16[4,576,128]{2,1,0:T(8,128)(2,1)S(1)}, u32[]{:S(2)}, u32[]{:S(2)}) collective-permute-start(bf16[4,576,128]{2,1,0:T(8,128)(2,1)S(1)} %shard_map.64.refs_5_), channel_id=1, source_target_pairs={{2,0},{4,2},{6,4},{3,1},{5,3},{7,5},{10,8},{12,10},{14,12},{11,9},... | collective-permute-start | bytes 1769480 | tf_op jit(solution)/shard_map/ppermute | solution.py:151
  24.2 16.6 %collective-permute-start.2 = (bf16[4,576,128]{2,1,0:T(8,128)(2,1)S(1)}, bf16[4,576,128]{2,1,0:T(8,128)(2,1)S(1)}, u32[]{:S(2)}, u32[]{:S(2)}) collective-permute-start(bf16[4,576,128]{2,1,0:T(8,128)(2,1)S(1)} %shard_map.64.refs_5_), channel_id=1, source_target_pairs={{0,2},{2,4},{4,6},{1,3},{3,5},{5,7},{8,10},{10,12},{12,14},{9,11},... | collective-permute-start | bytes 1769480 | tf_op jit(solution)/shard_map/ppermute | solution.py:151

commit v2 on v1

--- a/solution.py
+++ b/solution.py
@@ -20,9 +20,9 @@
     return 0.5 * x * (1.0 + lax.erf(x * 0.7071067811865476))
 
 
-def chunk_kernel(first, last, width, *refs):
+def chunk_kernel(bands, first, last, width, *refs):
     refs = list(refs)
-    lat_w, lon_w, gain, w_in, w_out, own, above, below = refs[:8]
+    lat_w, lon_w, gain, w_in, w_out, own, even_swap, odd_swap = refs[:8]
     refs = refs[8:]
     if not first:
         prev_own, prev_mix = refs[:2]
@@ -47,15 +47,21 @@
         mix[:, start + width :] = first_mix[...].astype(jnp.float32)
         state[:, start + width :] = first_own[:, : 2 * PAD]
 
+    band = lax.axis_index("band")
+    is_odd = lax.rem(band, 2) == 1
+    top, bottom = band == 0, band == bands - 1
     lat_tap = [jnp.broadcast_to(lat_w[k : k + 1], (PAD, channels)) for k in range(TAPS)]
 
     def mix_tile(t, carry):
         at = pl.multiple_of(t * PAD, PAD)
         to = pl.multiple_of(start + t * PAD, PAD)
-        strip = [above[r, pl.ds(at, PAD)] for r in range(REACH)]
+        evens = [even_swap[r, pl.ds(at, PAD)] for r in range(REACH)]
+        odds = [odd_swap[r, pl.ds(at, PAD)] for r in range(REACH)]
+        none = jnp.zeros_like(evens[0])
+        above = [jnp.where(top, none, jnp.where(is_odd, e, o)) for e, o in zip(evens, odds)]
+        below = [jnp.where(bottom, none, jnp.where(is_odd, o, e)) for e, o in zip(evens, odds)]
         mine = [own[r, pl.ds(at, PAD)] for r in range(rows)]
-        strip = strip + mine + [below[r, pl.ds(at, PAD)] for r in range(REACH)]
-        strip = [s.astype(jnp.float32) for s in strip]
+        strip = [s.astype(jnp.float32) for s in above + mine + below]
         for r in range(rows):
             total = strip[r] * lat_tap[0]
             for k in range(1, TAPS):
@@ -101,12 +107,12 @@
         rest(at, min(TILE, made - at))
 
 
-def layer_chunk(weights, chunk, prev, first_chunk, first, last):
-    own, above, below = chunk
+def layer_chunk(bands, weights, chunk, prev, first_chunk, first, last):
+    own, even_swap, odd_swap = chunk
     rows, width, channels = own.shape
     made = width + (0 if first else PAD) + (0 if last else -PAD) + (PAD if last else 0) - (PAD if first else 0)
     window = made + 2 * PAD
-    args = list(weights) + [own, above, below]
+    args = list(weights) + [own, even_swap, odd_swap]
     if not first:
         args += list(prev)
     if last and not first:
@@ -120,7 +126,7 @@
     cells = rows * made
     hidden = weights[3].shape[1]
     return pl.pallas_call(
-        functools.partial(chunk_kernel, first, last, width),
+        functools.partial(chunk_kernel, bands, first, last, width),
         out_shape=outs,
         in_specs=[pl.BlockSpec(memory_space=pltpu.VMEM)] * len(args),
         out_specs=[pl.BlockSpec(memory_space=pltpu.VMEM)] * len(outs),
@@ -141,20 +147,24 @@
     return [(lo, hi) for lo, hi in zip(edges[:-1], edges[1:])]
 
 
+def swaps(bands, start):
+    to = list(range(bands))
+    for b in range(start, bands - 1, 2):
+        to[b], to[b + 1] = b + 1, b
+    return list(enumerate(to))
+
+
 def member_step(state, weights, bands):
     rows, lons, _ = state.shape
-    up = [(b, b + 1) for b in range(bands - 1)]
-    down = [(b + 1, b) for b in range(bands - 1)]
+    even_pairs, odd_pairs = swaps(bands, 0), swaps(bands, 1)
+    assert rows == REACH
     chunks = [state[:, lo:hi] for lo, hi in splits(lons)]
     for layer in range(LAYERS):
-        halos = [
-            (lax.ppermute(own[rows - REACH :], "band", up), lax.ppermute(own[:REACH], "band", down))
-            for own in chunks
-        ]
+        halos = [(lax.ppermute(own, "band", even_pairs), lax.ppermute(own, "band", odd_pairs)) for own in chunks]
         made, prev, first_chunk = [], None, None
         for c, own in enumerate(chunks):
             first, last = c == 0, c == len(chunks) - 1
-            got = layer_chunk(weights[layer], (own,) + halos[c], prev, first_chunk, first, last)
+            got = layer_chunk(bands, weights[layer], (own,) + halos[c], prev, first_chunk, first, last)
             made.append(got[0])
             if not last:
                 prev = (own, got[1])

time: 45.2 us -> 43.9 us (0.971)
  starting transfers between devices: 13.2 us -> 10.9 us
  waiting for transfers between devices: 20.4 us -> 21.1 us
  Pallas kernels: 6.09 us -> 6.57 us
    ppermute x4, starting transfers between devices: 13.2 us -> 10.9 us  [the longest x2 8.32 us: member_step(): lax.ppermute(own, 'band', even_pairs)]
    ppermute x4, waiting for transfers between devices: 20.4 us -> 21.1 us  [the longest x2 21.1 us: member_step(): lax.ppermute(own, 'band', even_pairs)]
    pallas_call x2, Pallas kernels: 6.09 us -> 6.57 us  [layer_chunk(): pl.pallas_call(functools.partial(chunk_kernel, bands, first, last, width)...]
  transfers between devices with their start and end apart: 4 -> 4, of which waited for: 4 -> 2; matrix products, arithmetic and copies ran while one was open for 9% -> 9% of each run, Pallas kernels for 0% -> 0%
where the time goes in v2:
time: 43.9 us; the launch traced here: 43.6 us
  waiting for transfers between devices  21.1 us (48%)
  starting transfers between devices  10.9 us (25%)
  Pallas kernels  6.57 us (15%)
  local copies, waits for them, and re-layouts  4.12 us (9%)
  other arithmetic  0.86 us (2%)
    ppermute x2, waiting for transfers between devices, member_step(): lax.ppermute(own, 'band', even_pairs)  21.1 us
    ppermute x2, starting transfers between devices, member_step(): lax.ppermute(own, 'band', even_pairs)  8.32 us
    pallas_call x2, Pallas kernels, layer_chunk(): pl.pallas_call(functools.partial(chunk_kernel, bands, first, last, width)...  6.57 us
    ppermute x2, starting transfers between devices, member_step(): lax.ppermute(own, 'band', odd_pairs)  2.54 us
    squeeze x1, local copies, waits for them, and re-layouts, shards(): w_out[layer]  0.88 us
    squeeze x1, local copies, waits for them, and re-layouts, shards(): w_in[layer]  0.88 us
  transfers between devices with their start and end apart: 4, of which 2 were waited for; matrix products, arithmetic and copies ran while one was open for 9% of the time, Pallas kernels for 0%

profile of v2, /device:TPU:0, one launch (start us, length us, event | category | flops | bytes accessed | tf_op | source)
XLA Modules:
  0.0 43.6 jit_solution(5233545366401565483)
XLA Ops:
  0.0 0.0 copy-start
  0.0 1.8 %collective-permute-start.1 = (bf16[4,576,128]{2,1,0:T(8,128)(2,1)}, bf16[4,576,128]{2,1,0:T(8,128)(2,1)S(1)}, u32[]{:S(2)}, u32[]{:S(2)}) collective-permute-start(bf16[4,576,128]{2,1,0:T(8,128)(2,1)} %bitcast.31), channel_id=1, source_target_pairs={{0,0},{2,4},{4,2},{6,6},{1,1},{3,5},{5,3},{7,7},{8,8},{10,12},{12,... | collective-permute-start | bytes 1769480 | tf_op jit(solution)/shard_map/ppermute | solution.py:163
  1.8 4.9 %collective-permute-start = (bf16[4,576,128]{2,1,0:T(8,128)(2,1)}, bf16[4,576,128]{2,1,0:T(8,128)(2,1)S(1)}, u32[]{:S(2)}, u32[]{:S(2)}) collective-permute-start(bf16[4,576,128]{2,1,0:T(8,128)(2,1)} %bitcast.32), channel_id=1, source_target_pairs={{0,2},{2,0},{4,6},{6,4},{1,3},{3,1},{5,7},{7,5},{8,10},{10,8},{12,... | collective-permute-start | bytes 1769480 | tf_op jit(solution)/shard_map/ppermute | solution.py:163
  6.7 0.8 %fusion.5 = (bf16[1,9,128]{2,0,1:T(2,128)(2,1)S(1)}, bf16[1,9,128]{2,0,1:T(2,128)(2,1)S(1)}) fusion(bf16[2,9,128]{2,0,1:T(2,128)(2,1)} %param.7), kind=kLoop, calls=%fused_computation.14 | loop fusion | bytes 9216 | tf_op jit(solution)/shard_map/slice | solution.py:184
  7.5 0.8 %fusion.4 = (bf16[1,9,128]{2,0,1:T(2,128)(2,1)S(1)}, bf16[1,9,128]{2,0,1:T(2,128)(2,1)S(1)}) fusion(bf16[2,9,128]{2,0,1:T(2,128)(2,1)} %param.8), kind=kLoop, calls=%fused_computation.13 | loop fusion | bytes 9216 | tf_op jit(solution)/shard_map/slice | solution.py:185
  8.3 0.8 %fusion.6 = (f32[1,128]{1,0:T(1,128)S(1)}, f32[1,128]{1,0:T(1,128)S(1)}) fusion(f32[2,128]{1,0:T(2,128)} %param.9), kind=kLoop, calls=%fused_computation.15 | loop fusion | bytes 2048 | tf_op jit(solution)/shard_map/slice | solution.py:186
  9.0 0.9 %slice_bitcast_fusion.1 = (bf16[128,256]{1,0:T(8,128)(2,1)S(1)}, bf16[128,256]{1,0:T(8,128)(2,1)S(1)}) fusion(bf16[2,128,256]{2,1,0:T(8,128)(2,1)} %param.10), kind=kLoop, calls=%fused_computation.2 | loop fusion | bytes 262144 | tf_op jit(solution)/shard_map/squeeze | solution.py:187
  9.9 0.9 %slice_bitcast_fusion = (bf16[256,128]{1,0:T(8,128)(2,1)S(1)}, bf16[256,128]{1,0:T(8,128)(2,1)S(1)}) fusion(bf16[2,256,128]{2,1,0:T(8,128)(2,1)} %param.11), kind=kLoop, calls=%fused_computation.1 | loop fusion | bytes 262144 | tf_op jit(solution)/shard_map/squeeze | solution.py:188
  10.8 0.0 collective-permute-done.1.refs_7_
  10.8 9.1 %collective-permute-done.refs_6_ = bf16[4,576,128]{2,1,0:T(8,128)(2,1)S(1)} collective-permute-done((bf16[4,576,128]{2,1,0:T(8,128)(2,1)}, bf16[4,576,128]{2,1,0:T(8,128)(2,1)S(1)}, u32[]{:S(2)}, u32[]{:S(2)}) %collective-permute-start) | collective-permute-done | bytes 589856 | tf_op jit(solution)/shard_map/ppermute | solution.py:163
  20.0 0.0 copy-done
  20.0 3.3 %shard_map.64.refs_5_ = bf16[4,576,128]{2,1,0:T(8,128)(2,1)S(1)} custom-call(f32[9,128]{1,0:T(8,128)S(1)} %get-tuple-element.16.refs_0_, f32[9,128]{1,0:T(8,128)S(1)} %get-tuple-element.15.refs_1_, f32[1,128]{1,0:T(1,128)S(1)} %get-tuple-element.13.refs_2_, bf16[128,256]{1,0:T(8,128)(2,1)S(1)} %get-tuple-element.7.refs_3_, ...), custom_call_target="tpu_custom_call" | custom-call | flops 301989888 | bytes 2359296 | tf_op jit(solution)/shard_map/pallas_call | solution.py:128
  23.3 0.7 %collective-permute-start.3 = (bf16[4,576,128]{2,1,0:T(8,128)(2,1)S(1)}, bf16[4,576,128]{2,1,0:T(8,128)(2,1)S(1)}, u32[]{:S(2)}, u32[]{:S(2)}) collective-permute-start(bf16[4,576,128]{2,1,0:T(8,128)(2,1)S(1)} %shard_map.64.refs_5_), channel_id=1, source_target_pairs={{0,0},{2,4},{4,2},{6,6},{1,1},{3,5},{5,3},{7,7},{8,8},{10,12},{12,... | collective-permute-start | bytes 1769480 | tf_op jit(solution)/shard_map/ppermute | solution.py:163
  24.0 3.5 %collective-permute-start.2 = (bf16[4,576,128]{2,1,0:T(8,128)(2,1)S(1)}, bf16[4,576,128]{2,1,0:T(8,128)(2,1)S(1)}, u32[]{:S(2)}, u32[]{:S(2)}) collective-permute-start(bf16[4,576,128]{2,1,0:T(8,128)(2,1)S(1)} %shard_map.64.refs_5_), channel_id=1, source_target_pairs={{0,2},{2,0},{4,6},{6,4},{1,3},{3,1},{5,7},{7,5},{8,10},{10,8},{12,... | collective-permute-start | bytes 1769480 | tf_op jit(solution)/shard_map/ppermute | solution.py:163
  27.4 0.0 collective-permute-done.3.refs_7_
  27.4 11.9 %collective-permute-done.2.refs_6_ = bf16[4,576,128]{2,1,0:T(8,128)(2,1)S(1)} collective-permute-done((bf16[4,576,128]{2,1,0:T(8,128)(2,1)S(1)}, bf16[4,576,128]{2,1,0:T(8,128)(2,1)S(1)}, u32[]{:S(2)}, u32[]{:S(2)}) %collective-permute-start.2) | collective-permute-done | bytes 589856 | tf_op jit(solution)/shard_map/ppermute | solution.py:163
  39.4 3.3 %shard_map.65 = bf16[4,576,128]{2,1,0:T(8,128)(2,1)S(1)} custom-call(f32[9,128]{1,0:T(8,128)S(1)} %get-tuple-element.18.refs_0_, f32[9,128]{1,0:T(8,128)S(1)} %get-tuple-element.17.refs_1_, f32[1,128]{1,0:T(1,128)S(1)} %get-tuple-element.14.refs_2_, bf16[128,256]{1,0:T(8,128)(2,1)S(1)} %get-tuple-element.8.refs_3_, ...), custom_call_target="tpu_custom_call" | custom-call | flops 301989888 | bytes 2359296 | tf_op jit(solution)/shard_map/pallas_call | solution.py:128
  42.7 0.9 %maximum_bitcast_fusion = bf16[1,4,576,128]{3,2,1,0:T(8,128)(2,1)} fusion(bf16[4,544,128]{2,1,0:T(8,128)(2,1)S(1)} %slice.51, bf16[4,32,128]{2,1,0:T(8,128)(2,1)S(1)} %slice.50), kind=kLoop, calls=%fused_computation | loop fusion | flops 1179648 | bytes 1179648 | tf_op jit(solution)/shard_map/stack | solution.py:192
  (4 shorter events, 0.1 us)
Async XLA Ops:
  0.0 20.0 %copy-start = (bf16[1,4,576,128]{3,2,1,0:T(8,128)(2,1)S(1)}, bf16[1,4,576,128]{3,2,1,0:T(8,128)(2,1)}, u32[]{:S(2)}) copy-start(bf16[1,4,576,128]{3,2,1,0:T(8,128)(2,1)} %param.6) | copy-start | bytes 1769476
  0.0 10.8 %collective-permute-start.1 = (bf16[4,576,128]{2,1,0:T(8,128)(2,1)}, bf16[4,576,128]{2,1,0:T(8,128)(2,1)S(1)}, u32[]{:S(2)}, u32[]{:S(2)}) collective-permute-start(bf16[4,576,128]{2,1,0:T(8,128)(2,1)} %bitcast.31), channel_id=1, source_target_pairs={{0,0},{2,4},{4,2},{6,6},{1,1},{3,5},{5,3},{7,7},{8,8},{10,12},{12,... | collective-permute-start | bytes 1769480 | tf_op jit(solution)/shard_map/ppermute | solution.py:163
  1.8 18.1 %collective-permute-start = (bf16[4,576,128]{2,1,0:T(8,128)(2,1)}, bf16[4,576,128]{2,1,0:T(8,128)(2,1)S(1)}, u32[]{:S(2)}, u32[]{:S(2)}) collective-permute-start(bf16[4,576,128]{2,1,0:T(8,128)(2,1)} %bitcast.32), channel_id=1, source_target_pairs={{0,2},{2,0},{4,6},{6,4},{1,3},{3,1},{5,7},{7,5},{8,10},{10,8},{12,... | collective-permute-start | bytes 1769480 | tf_op jit(solution)/shard_map/ppermute | solution.py:163
  23.3 4.2 %collective-permute-start.3 = (bf16[4,576,128]{2,1,0:T(8,128)(2,1)S(1)}, bf16[4,576,128]{2,1,0:T(8,128)(2,1)S(1)}, u32[]{:S(2)}, u32[]{:S(2)}) collective-permute-start(bf16[4,576,128]{2,1,0:T(8,128)(2,1)S(1)} %shard_map.64.refs_5_), channel_id=1, source_target_pairs={{0,0},{2,4},{4,2},{6,6},{1,1},{3,5},{5,3},{7,7},{8,8},{10,12},{12,... | collective-permute-start | bytes 1769480 | tf_op jit(solution)/shard_map/ppermute | solution.py:163
  24.0 15.4 %collective-permute-start.2 = (bf16[4,576,128]{2,1,0:T(8,128)(2,1)S(1)}, bf16[4,576,128]{2,1,0:T(8,128)(2,1)S(1)}, u32[]{:S(2)}, u32[]{:S(2)}) collective-permute-start(bf16[4,576,128]{2,1,0:T(8,128)(2,1)S(1)} %shard_map.64.refs_5_), channel_id=1, source_target_pairs={{0,2},{2,0},{4,6},{6,4},{1,3},{3,1},{5,7},{7,5},{8,10},{10,8},{12,... | collective-permute-start | bytes 1769480 | tf_op jit(solution)/shard_map/ppermute | solution.py:163

commit v3 on v2

--- a/solution.py
+++ b/solution.py
@@ -12,7 +12,7 @@
 TAPS = 9
 REACH = TAPS // 2
 PAD = 16
-CHUNKS = 1
+CHUNKS = 2
 TILE = 32
 
 

time: 43.9 us -> 43.8 us (level)
  the two profiles are of different devices: /device:TPU:0 before, /device:TPU:14 now
where the time goes in v3:
time: 43.8 us; the launch traced here: 43.6 us
  waiting for transfers between devices  19.8 us (45%)
  starting transfers between devices  13.5 us (31%)
  Pallas kernels  7.08 us (16%)
  local copies, waits for them, and re-layouts  2.02 us (5%)
  other arithmetic  0.87 us (2%)
    ppermute x4, waiting for transfers between devices, member_step(): lax.ppermute(own, 'band', even_pairs)  14.9 us
    ppermute x4, starting transfers between devices, member_step(): lax.ppermute(own, 'band', odd_pairs)  12.8 us
    pallas_call x4, Pallas kernels, layer_chunk(): pl.pallas_call(functools.partial(chunk_kernel, bands, first, last, width)...  7.08 us
    ppermute x4, waiting for transfers between devices, member_step(): lax.ppermute(own, 'band', odd_pairs)  4.93 us
    slice x1, local copies, waits for them, and re-layouts, member_step(): chunks = [state[:, lo:hi] for lo, hi in splits(lons)]  1.18 us
  transfers between devices with their start and end apart: 8, of which 4 were waited for; matrix products, arithmetic and copies ran while one was open for 2% of the time, Pallas kernels for 7%

profile of v3, /device:TPU:14, one launch (start us, length us, event | category | flops | bytes accessed | tf_op | source)
XLA Modules:
  0.0 43.6 jit_solution(3144793863104827152)
XLA Ops:
  0.0 0.0 copy-start.4
  0.0 1.2 %fusion.6 = (bf16[4,288,128]{2,1,0:T(8,128)(2,1)S(1)}, bf16[4,288,128]{2,1,0:T(8,128)(2,1)S(1)}) fusion(bf16[4,576,128]{2,1,0:T(8,128)(2,1)} %bitcast.31), kind=kLoop, calls=%fused_computation.15 | loop fusion | bytes 1179648 | tf_op jit(solution)/shard_map/slice | solution.py:161
  1.2 0.5 %collective-permute-start = (bf16[4,288,128]{2,1,0:T(8,128)(2,1)S(1)}, bf16[4,288,128]{2,1,0:T(8,128)(2,1)S(1)}, u32[]{:S(2)}, u32[]{:S(2)}) collective-permute-start(bf16[4,288,128]{2,1,0:T(8,128)(2,1)S(1)} %get-tuple-element.18.refs_5_), channel_id=1, source_target_pairs={{0,2},{2,0},{4,6},{6,4},{1,3},{3,1},{5,7},{7,5},{8,10},{10,8},{12,... | collective-permute-start | bytes 884744 | tf_op jit(solution)/shard_map/ppermute | solution.py:163
  1.7 4.6 %collective-permute-start.1 = (bf16[4,288,128]{2,1,0:T(8,128)(2,1)S(1)}, bf16[4,288,128]{2,1,0:T(8,128)(2,1)S(1)}, u32[]{:S(2)}, u32[]{:S(2)}) collective-permute-start(bf16[4,288,128]{2,1,0:T(8,128)(2,1)S(1)} %get-tuple-element.18.refs_5_), channel_id=1, source_target_pairs={{0,0},{2,4},{4,2},{6,6},{1,1},{3,5},{5,3},{7,7},{8,8},{10,12},{12,... | collective-permute-start | bytes 884744 | tf_op jit(solution)/shard_map/ppermute | solution.py:163
  6.3 0.1 collective-permute-start.2
  6.4 1.9 %collective-permute-start.3 = (bf16[4,288,128]{2,1,0:T(8,128)(2,1)S(1)}, bf16[4,288,128]{2,1,0:T(8,128)(2,1)S(1)}, u32[]{:S(2)}, u32[]{:S(2)}) collective-permute-start(bf16[4,288,128]{2,1,0:T(8,128)(2,1)S(1)} %get-tuple-element.17.refs_5_.refs_8_), channel_id=1, source_target_pairs={{0,0},{2,4},{4,2},{6,6},{1,1},{3,5},{5,3},{7,7},{8,8},{10,12},{12,... | collective-permute-start | bytes 884744 | tf_op jit(solution)/shard_map/ppermute | solution.py:163
  8.5 0.8 %slice.70.refs_10_ = bf16[4,32,128]{2,1,0:T(8,128)(2,1)S(1)} slice(bf16[4,576,128]{2,1,0:T(8,128)(2,1)} %bitcast.32), slice={[0:4], [0:32], [0:128]} | slice | bytes 65536 | tf_op jit(solution)/shard_map/slice | solution.py:172
  9.2 7.1 %collective-permute-done.2.refs_6_ = bf16[4,288,128]{2,1,0:T(8,128)(2,1)S(1)} collective-permute-done((bf16[4,288,128]{2,1,0:T(8,128)(2,1)S(1)}, bf16[4,288,128]{2,1,0:T(8,128)(2,1)S(1)}, u32[]{:S(2)}, u32[]{:S(2)}) %collective-permute-start.2) | collective-permute-done | bytes 294944 | tf_op jit(solution)/shard_map/ppermute | solution.py:163
  16.3 3.0 %collective-permute-done.3.refs_7_ = bf16[4,288,128]{2,1,0:T(8,128)(2,1)S(1)} collective-permute-done((bf16[4,288,128]{2,1,0:T(8,128)(2,1)S(1)}, bf16[4,288,128]{2,1,0:T(8,128)(2,1)S(1)}, u32[]{:S(2)}, u32[]{:S(2)}) %collective-permute-start.3) | collective-permute-done | bytes 294944 | tf_op jit(solution)/shard_map/ppermute | solution.py:163
  19.4 1.7 %shard_map.64 = (bf16[4,256,128]{2,1,0:T(8,128)(2,1)S(1)}, bf16[4,32,128]{2,1,0:T(8,128)(2,1)S(1)}, bf16[4,32,128]{2,1,0:T(8,128)(2,1)S(1)}) custom-call(f32[9,128]{1,0:T(8,128)S(1)} %get-tuple-element.30.refs_0_, f32[9,128]{1,0:T(8,128)S(1)} %get-tuple-element.29.refs_1_, f32[1,128]{1,0:T(1,128)S(1)} %get-tuple-element.27.refs_2_, ...), custom_call_target="tpu_custom_call" | custom-call | flops 134217728 | bytes 1048576 | tf_op jit(solution)/shard_map/pallas_call | solution.py:128
  21.1 0.0 collective-permute-done.refs_6_
  21.1 0.0 collective-permute-done.1.refs_7_
  21.1 1.9 %shard_map.65.refs_5_ = bf16[4,320,128]{2,1,0:T(8,128)(2,1)S(1)} custom-call(f32[9,128]{1,0:T(8,128)S(1)} %get-tuple-element.30.refs_0_, f32[9,128]{1,0:T(8,128)S(1)} %get-tuple-element.29.refs_1_, f32[1,128]{1,0:T(1,128)S(1)} %get-tuple-element.27.refs_2_, bf16[128,256]{1,0:T(8,128)(2,1)S(1)} %get-tuple-element.21.refs_3_, ...), custom_call_target="tpu_custom_call" | custom-call | flops 167772160 | bytes 1310720 | tf_op jit(solution)/shard_map/pallas_call | solution.py:128
  23.0 0.1 collective-permute-start.4
  23.0 3.6 %collective-permute-start.5 = (bf16[4,320,128]{2,1,0:T(8,128)(2,1)S(1)}, bf16[4,320,128]{2,1,0:T(8,128)(2,1)S(1)}, u32[]{:S(2)}, u32[]{:S(2)}) collective-permute-start(bf16[4,320,128]{2,1,0:T(8,128)(2,1)S(1)} %shard_map.65.refs_5_), channel_id=1, source_target_pairs={{0,0},{2,4},{4,2},{6,6},{1,1},{3,5},{5,3},{7,7},{8,8},{10,12},{12,... | collective-permute-start | bytes 983048 | tf_op jit(solution)/shard_map/ppermute | solution.py:163
  26.7 0.1 collective-permute-start.6
  26.8 2.7 %collective-permute-start.7 = (bf16[4,256,128]{2,1,0:T(8,128)(2,1)S(1)}, bf16[4,256,128]{2,1,0:T(8,128)(2,1)S(1)}, u32[]{:S(2)}, u32[]{:S(2)}) collective-permute-start(bf16[4,256,128]{2,1,0:T(8,128)(2,1)S(1)} %get-tuple-element.13.refs_5_.refs_8_), channel_id=1, source_target_pairs={{0,0},{2,4},{4,2},{6,6},{1,1},{3,5},{5,3},{7,7},{8,8},{10,12},{12,... | collective-permute-start | bytes 786440 | tf_op jit(solution)/shard_map/ppermute | solution.py:163
  29.5 7.8 %collective-permute-done.6.refs_6_ = bf16[4,256,128]{2,1,0:T(8,128)(2,1)S(1)} collective-permute-done((bf16[4,256,128]{2,1,0:T(8,128)(2,1)S(1)}, bf16[4,256,128]{2,1,0:T(8,128)(2,1)S(1)}, u32[]{:S(2)}, u32[]{:S(2)}) %collective-permute-start.6) | collective-permute-done | bytes 262176 | tf_op jit(solution)/shard_map/ppermute | solution.py:163
  37.2 1.9 %collective-permute-done.7.refs_7_ = bf16[4,256,128]{2,1,0:T(8,128)(2,1)S(1)} collective-permute-done((bf16[4,256,128]{2,1,0:T(8,128)(2,1)S(1)}, bf16[4,256,128]{2,1,0:T(8,128)(2,1)S(1)}, u32[]{:S(2)}, u32[]{:S(2)}) %collective-permute-start.7) | collective-permute-done | bytes 262176 | tf_op jit(solution)/shard_map/ppermute | solution.py:163
  39.1 1.5 %shard_map.66 = (bf16[4,224,128]{2,1,0:T(8,128)(2,1)S(1)}, bf16[4,32,128]{2,1,0:T(8,128)(2,1)S(1)}, bf16[4,32,128]{2,1,0:T(8,128)(2,1)S(1)}) custom-call(f32[9,128]{1,0:T(8,128)S(1)} %get-tuple-element.32.refs_0_, f32[9,128]{1,0:T(8,128)S(1)} %get-tuple-element.31.refs_1_, f32[1,128]{1,0:T(1,128)S(1)} %get-tuple-element.28.refs_2_, ...), custom_call_target="tpu_custom_call" | custom-call | flops 117440512 | bytes 917504 | tf_op jit(solution)/shard_map/pallas_call | solution.py:128
  40.6 0.0 collective-permute-done.4.refs_6_
  40.6 0.0 collective-permute-done.5.refs_7_
  40.6 2.0 %shard_map.67 = bf16[4,352,128]{2,1,0:T(8,128)(2,1)S(1)} custom-call(f32[9,128]{1,0:T(8,128)S(1)} %get-tuple-element.32.refs_0_, f32[9,128]{1,0:T(8,128)S(1)} %get-tuple-element.31.refs_1_, f32[1,128]{1,0:T(1,128)S(1)} %get-tuple-element.28.refs_2_, bf16[128,256]{1,0:T(8,128)(2,1)S(1)} %get-tuple-element.22.refs_3_, ...), custom_call_target="tpu_custom_call" | custom-call | flops 184549376 | bytes 1441792 | tf_op jit(solution)/shard_map/pallas_call | solution.py:128
  42.7 0.9 %fusion.1 = bf16[1,4,576,128]{3,2,1,0:T(8,128)(2,1)} fusion(bf16[4,352,128]{2,1,0:T(8,128)(2,1)S(1)} %shard_map.67, bf16[4,224,128]{2,1,0:T(8,128)(2,1)S(1)} %get-tuple-element.16, bf16[4,32,128]{2,1,0:T(8,128)(2,1)S(1)} %slice.71), kind=kLoop, calls=%fused_computation.2 | loop fusion | flops 1769472 | bytes 1212416 | tf_op jit(solution)/shard_map/stack | solution.py:192
  (18 shorter events, 0.1 us)
Async XLA Ops:
  0.0 8.3 %copy-start.2 = (bf16[2,9,128]{2,0,1:T(2,128)(2,1)S(1)}, bf16[2,9,128]{2,0,1:T(2,128)(2,1)}, u32[]{:S(2)}) copy-start(bf16[2,9,128]{2,0,1:T(2,128)(2,1)} %param.8) | copy-start | bytes 13828
  0.0 8.4 %copy-start.3 = (bf16[2,9,128]{2,0,1:T(2,128)(2,1)S(1)}, bf16[2,9,128]{2,0,1:T(2,128)(2,1)}, u32[]{:S(2)}) copy-start(bf16[2,9,128]{2,0,1:T(2,128)(2,1)} %param.7) | copy-start | bytes 13828
  0.0 8.4 %copy-start = (bf16[2,128,256]{2,1,0:T(8,128)(2,1)S(1)}, bf16[2,128,256]{2,1,0:T(8,128)(2,1)}, u32[]{:S(2)}) copy-start(bf16[2,128,256]{2,1,0:T(8,128)(2,1)} %param.10) | copy-start | bytes 393220
  0.0 8.4 %copy-start.4 = (f32[2,128]{1,0:T(2,128)S(1)}, f32[2,128]{1,0:T(2,128)}, u32[]{:S(2)}) copy-start(f32[2,128]{1,0:T(2,128)} %param.9) | copy-start | bytes 3076
  0.0 9.2 %copy-start.1 = (bf16[2,256,128]{2,1,0:T(8,128)(2,1)S(1)}, bf16[2,256,128]{2,1,0:T(8,128)(2,1)}, u32[]{:S(2)}) copy-start(bf16[2,256,128]{2,1,0:T(8,128)(2,1)} %param.11) | copy-start | bytes 393220
  1.2 19.8 %collective-permute-start = (bf16[4,288,128]{2,1,0:T(8,128)(2,1)S(1)}, bf16[4,288,128]{2,1,0:T(8,128)(2,1)S(1)}, u32[]{:S(2)}, u32[]{:S(2)}) collective-permute-start(bf16[4,288,128]{2,1,0:T(8,128)(2,1)S(1)} %get-tuple-element.18.refs_5_), channel_id=1, source_target_pairs={{0,2},{2,0},{4,6},{6,4},{1,3},{3,1},{5,7},{7,5},{8,10},{10,8},{12,... | collective-permute-start | bytes 884744 | tf_op jit(solution)/shard_map/ppermute | solution.py:163
  1.7 19.3 %collective-permute-start.1 = (bf16[4,288,128]{2,1,0:T(8,128)(2,1)S(1)}, bf16[4,288,128]{2,1,0:T(8,128)(2,1)S(1)}, u32[]{:S(2)}, u32[]{:S(2)}) collective-permute-start(bf16[4,288,128]{2,1,0:T(8,128)(2,1)S(1)} %get-tuple-element.18.refs_5_), channel_id=1, source_target_pairs={{0,0},{2,4},{4,2},{6,6},{1,1},{3,5},{5,3},{7,7},{8,8},{10,12},{12,... | collective-permute-start | bytes 884744 | tf_op jit(solution)/shard_map/ppermute | solution.py:163
  6.3 10.0 %collective-permute-start.2 = (bf16[4,288,128]{2,1,0:T(8,128)(2,1)S(1)}, bf16[4,288,128]{2,1,0:T(8,128)(2,1)S(1)}, u32[]{:S(2)}, u32[]{:S(2)}) collective-permute-start(bf16[4,288,128]{2,1,0:T(8,128)(2,1)S(1)} %get-tuple-element.17.refs_5_.refs_8_), channel_id=1, source_target_pairs={{0,2},{2,0},{4,6},{6,4},{1,3},{3,1},{5,7},{7,5},{8,10},{10,8},{12,... | collective-permute-start | bytes 884744 | tf_op jit(solution)/shard_map/ppermute | solution.py:163
  6.4 13.0 %collective-permute-start.3 = (bf16[4,288,128]{2,1,0:T(8,128)(2,1)S(1)}, bf16[4,288,128]{2,1,0:T(8,128)(2,1)S(1)}, u32[]{:S(2)}, u32[]{:S(2)}) collective-permute-start(bf16[4,288,128]{2,1,0:T(8,128)(2,1)S(1)} %get-tuple-element.17.refs_5_.refs_8_), channel_id=1, source_target_pairs={{0,0},{2,4},{4,2},{6,6},{1,1},{3,5},{5,3},{7,7},{8,8},{10,12},{12,... | collective-permute-start | bytes 884744 | tf_op jit(solution)/shard_map/ppermute | solution.py:163
  23.0 17.7 %collective-permute-start.4 = (bf16[4,320,128]{2,1,0:T(8,128)(2,1)S(1)}, bf16[4,320,128]{2,1,0:T(8,128)(2,1)S(1)}, u32[]{:S(2)}, u32[]{:S(2)}) collective-permute-start(bf16[4,320,128]{2,1,0:T(8,128)(2,1)S(1)} %shard_map.65.refs_5_), channel_id=1, source_target_pairs={{0,2},{2,0},{4,6},{6,4},{1,3},{3,1},{5,7},{7,5},{8,10},{10,8},{12,... | collective-permute-start | bytes 983048 | tf_op jit(solution)/shard_map/ppermute | solution.py:163
  23.0 17.6 %collective-permute-start.5 = (bf16[4,320,128]{2,1,0:T(8,128)(2,1)S(1)}, bf16[4,320,128]{2,1,0:T(8,128)(2,1)S(1)}, u32[]{:S(2)}, u32[]{:S(2)}) collective-permute-start(bf16[4,320,128]{2,1,0:T(8,128)(2,1)S(1)} %shard_map.65.refs_5_), channel_id=1, source_target_pairs={{0,0},{2,4},{4,2},{6,6},{1,1},{3,5},{5,3},{7,7},{8,8},{10,12},{12,... | collective-permute-start | bytes 983048 | tf_op jit(solution)/shard_map/ppermute | solution.py:163
  26.7 10.5 %collective-permute-start.6 = (bf16[4,256,128]{2,1,0:T(8,128)(2,1)S(1)}, bf16[4,256,128]{2,1,0:T(8,128)(2,1)S(1)}, u32[]{:S(2)}, u32[]{:S(2)}) collective-permute-start(bf16[4,256,128]{2,1,0:T(8,128)(2,1)S(1)} %get-tuple-element.13.refs_5_.refs_8_), channel_id=1, source_target_pairs={{0,2},{2,0},{4,6},{6,4},{1,3},{3,1},{5,7},{7,5},{8,10},{10,8},{12,... | collective-permute-start | bytes 786440 | tf_op jit(solution)/shard_map/ppermute | solution.py:163
  26.8 12.4 %collective-permute-start.7 = (bf16[4,256,128]{2,1,0:T(8,128)(2,1)S(1)}, bf16[4,256,128]{2,1,0:T(8,128)(2,1)S(1)}, u32[]{:S(2)}, u32[]{:S(2)}) collective-permute-start(bf16[4,256,128]{2,1,0:T(8,128)(2,1)S(1)} %get-tuple-element.13.refs_5_.refs_8_), channel_id=1, source_target_pairs={{0,0},{2,4},{4,2},{6,6},{1,1},{3,5},{5,3},{7,7},{8,8},{10,12},{12,... | collective-permute-start | bytes 786440 | tf_op jit(solution)/shard_map/ppermute | solution.py:163

commit v4 on v3

--- a/solution.py
+++ b/solution.py
@@ -12,7 +12,6 @@
 TAPS = 9
 REACH = TAPS // 2
 PAD = 16
-CHUNKS = 2
 TILE = 32
 
 
@@ -136,15 +135,14 @@
         ],
         compiler_params=pltpu.CompilerParams(vmem_limit_bytes=24 * 2**20),
         cost_estimate=pl.CostEstimate(
-            flops=4 * cells * channels * hidden, bytes_accessed=8 * cells * channels, transcendentals=cells * hidden
+            flops=50 * cells * channels * hidden, bytes_accessed=8 * cells * channels, transcendentals=cells * hidden
         ),
     )(*args)
 
 
 def splits(total):
-    tiles = total // PAD
-    edges = [PAD * ((tiles * c) // CHUNKS) for c in range(CHUNKS)] + [total]
-    return [(lo, hi) for lo, hi in zip(edges[:-1], edges[1:])]
+    first = PAD * ((total // PAD + 4 * LAYERS) // 2)
+    return [(0, first), (first, total)]
 
 
 def swaps(bands, start):

time: 43.8 us -> 35.5 us (0.81)
  the two profiles are of different devices: /device:TPU:14 before, /device:TPU:16 now
where the time goes in v4:
time: 35.5 us; the launch traced here: 35.2 us
  starting transfers between devices  13.5 us (38%)
  waiting for transfers between devices  10.6 us (30%)
  Pallas kernels  7.11 us (20%)
  local copies, waits for them, and re-layouts  2.88 us (8%)
  other arithmetic  0.87 us (2%)
    ppermute x4, starting transfers between devices, member_step(): lax.ppermute(own, 'band', odd_pairs)  10.9 us
    pallas_call x4, Pallas kernels, layer_chunk(): pl.pallas_call(functools.partial(chunk_kernel, bands, first, last, width)...  7.11 us
    ppermute x4, waiting for transfers between devices, member_step(): lax.ppermute(own, 'band', odd_pairs)  6.36 us
    ppermute x4, waiting for transfers between devices, member_step(): lax.ppermute(own, 'band', even_pairs)  4.26 us
    ppermute x4, starting transfers between devices, member_step(): lax.ppermute(own, 'band', even_pairs)  2.61 us
    slice x2, local copies, waits for them, and re-layouts, member_step(): chunks = [state[:, lo:hi] for lo, hi in splits(lons)]  2.03 us
    another operation x1, other arithmetic, shards(): jnp.stack([member_step(fields[m], weights, bands) for m in range(fields.s...  0.86 us
    slice x2, local copies, waits for them, and re-layouts, member_step(): first_chunk = (own[:, :2 * PAD], got[2])  0.77 us
  transfers between devices with their start and end apart: 8, of which 5 were waited for; matrix products, arithmetic and copies ran while one was open for 5% of the time, Pallas kernels for 15%

profile of v4, /device:TPU:16, one launch (start us, length us, event | category | flops | bytes accessed | tf_op | source)
XLA Modules:
  0.0 35.2 jit_solution(8082020357164253516)
XLA Ops:
  0.0 1.1 %slice.69.refs_5_.refs_8_ = bf16[4,352,128]{2,1,0:T(8,128)(2,1)S(1)} slice(bf16[4,576,128]{2,1,0:T(8,128)(2,1)} %bitcast.31), slice={[0:4], [0:352], [0:128]} | slice | bytes 720896 | tf_op jit(solution)/shard_map/slice | solution.py:159
  1.1 0.0 copy-start.4
  1.1 1.6 %collective-permute-start.2 = (bf16[4,352,128]{2,1,0:T(8,128)(2,1)S(1)}, bf16[4,352,128]{2,1,0:T(8,128)(2,1)S(1)}, u32[]{:S(2)}, u32[]{:S(2)}) collective-permute-start(bf16[4,352,128]{2,1,0:T(8,128)(2,1)S(1)} %slice.69.refs_5_.refs_8_), channel_id=1, source_target_pairs={{0,2},{2,0},{4,6},{6,4},{1,3},{3,1},{5,7},{7,5},{8,10},{10,8},{12,... | collective-permute-start | bytes 1081352 | tf_op jit(solution)/shard_map/ppermute | solution.py:161
  2.7 1.9 %collective-permute-start.3 = (bf16[4,352,128]{2,1,0:T(8,128)(2,1)S(1)}, bf16[4,352,128]{2,1,0:T(8,128)(2,1)S(1)}, u32[]{:S(2)}, u32[]{:S(2)}) collective-permute-start(bf16[4,352,128]{2,1,0:T(8,128)(2,1)S(1)} %slice.69.refs_5_.refs_8_), channel_id=1, source_target_pairs={{0,0},{2,4},{4,2},{6,6},{1,1},{3,5},{5,3},{7,7},{8,8},{10,12},{12,... | collective-permute-start | bytes 1081352 | tf_op jit(solution)/shard_map/ppermute | solution.py:161
  4.7 1.0 %slice.68.refs_5_ = bf16[4,224,128]{2,1,0:T(8,128)(2,1)S(1)} slice(bf16[4,576,128]{2,1,0:T(8,128)(2,1)} %bitcast.32), slice={[0:4], [352:576], [0:128]} | slice | bytes 458752 | tf_op jit(solution)/shard_map/slice | solution.py:159
  5.6 0.1 collective-permute-start
  5.7 3.9 %collective-permute-start.1 = (bf16[4,224,128]{2,1,0:T(8,128)(2,1)S(1)}, bf16[4,224,128]{2,1,0:T(8,128)(2,1)S(1)}, u32[]{:S(2)}, u32[]{:S(2)}) collective-permute-start(bf16[4,224,128]{2,1,0:T(8,128)(2,1)S(1)} %slice.68.refs_5_), channel_id=1, source_target_pairs={{0,0},{2,4},{4,2},{6,6},{1,1},{3,5},{5,3},{7,7},{8,8},{10,12},{12,... | collective-permute-start | bytes 688136 | tf_op jit(solution)/shard_map/ppermute | solution.py:161
  9.8 0.8 %slice.70.refs_10_ = bf16[4,32,128]{2,1,0:T(8,128)(2,1)S(1)} slice(bf16[4,576,128]{2,1,0:T(8,128)(2,1)} %bitcast.33), slice={[0:4], [0:32], [0:128]} | slice | bytes 65536 | tf_op jit(solution)/shard_map/slice | solution.py:170
  10.6 1.9 %collective-permute-done.2.refs_6_ = bf16[4,352,128]{2,1,0:T(8,128)(2,1)S(1)} collective-permute-done((bf16[4,352,128]{2,1,0:T(8,128)(2,1)S(1)}, bf16[4,352,128]{2,1,0:T(8,128)(2,1)S(1)}, u32[]{:S(2)}, u32[]{:S(2)}) %collective-permute-start.2) | collective-permute-done | bytes 360480 | tf_op jit(solution)/shard_map/ppermute | solution.py:161
  12.5 3.5 %collective-permute-done.3.refs_7_ = bf16[4,352,128]{2,1,0:T(8,128)(2,1)S(1)} collective-permute-done((bf16[4,352,128]{2,1,0:T(8,128)(2,1)S(1)}, bf16[4,352,128]{2,1,0:T(8,128)(2,1)S(1)}, u32[]{:S(2)}, u32[]{:S(2)}) %collective-permute-start.3) | collective-permute-done | bytes 360480 | tf_op jit(solution)/shard_map/ppermute | solution.py:161
  16.0 2.0 %shard_map.64 = (bf16[4,320,128]{2,1,0:T(8,128)(2,1)S(1)}, bf16[4,32,128]{2,1,0:T(8,128)(2,1)S(1)}, bf16[4,32,128]{2,1,0:T(8,128)(2,1)S(1)}) custom-call(f32[9,128]{1,0:T(8,128)S(1)} %get-tuple-element.28.refs_0_, f32[9,128]{1,0:T(8,128)S(1)} %get-tuple-element.27.refs_1_, f32[1,128]{1,0:T(1,128)S(1)} %get-tuple-element.25.refs_2_, ...), custom_call_target="tpu_custom_call" | custom-call | flops 2097152000 | bytes 1310720 | tf_op jit(solution)/shard_map/pallas_call | solution.py:127
  18.0 0.1 collective-permute-start.6
  18.1 1.9 %collective-permute-start.7 = (bf16[4,320,128]{2,1,0:T(8,128)(2,1)S(1)}, bf16[4,320,128]{2,1,0:T(8,128)(2,1)S(1)}, u32[]{:S(2)}, u32[]{:S(2)}) collective-permute-start(bf16[4,320,128]{2,1,0:T(8,128)(2,1)S(1)} %get-tuple-element.13.refs_5_.refs_8_), channel_id=1, source_target_pairs={{0,0},{2,4},{4,2},{6,6},{1,1},{3,5},{5,3},{7,7},{8,8},{10,12},{12,... | collective-permute-start | bytes 983048 | tf_op jit(solution)/shard_map/ppermute | solution.py:161
  20.0 0.0 collective-permute-done.refs_6_
  20.0 1.5 %shard_map.65.refs_5_ = bf16[4,256,128]{2,1,0:T(8,128)(2,1)S(1)} custom-call(f32[9,128]{1,0:T(8,128)S(1)} %get-tuple-element.28.refs_0_, f32[9,128]{1,0:T(8,128)S(1)} %get-tuple-element.27.refs_1_, f32[1,128]{1,0:T(1,128)S(1)} %get-tuple-element.25.refs_2_, bf16[128,256]{1,0:T(8,128)(2,1)S(1)} %get-tuple-element.19.refs_3_, ...), custom_call_target="tpu_custom_call" | custom-call | flops 1677721600 | bytes 1048576 | tf_op jit(solution)/shard_map/pallas_call | solution.py:127
  21.6 0.8 %collective-permute-start.4 = (bf16[4,256,128]{2,1,0:T(8,128)(2,1)S(1)}, bf16[4,256,128]{2,1,0:T(8,128)(2,1)S(1)}, u32[]{:S(2)}, u32[]{:S(2)}) collective-permute-start(bf16[4,256,128]{2,1,0:T(8,128)(2,1)S(1)} %shard_map.65.refs_5_), channel_id=1, source_target_pairs={{0,2},{2,0},{4,6},{6,4},{1,3},{3,1},{5,7},{7,5},{8,10},{10,8},{12,... | collective-permute-start | bytes 786440 | tf_op jit(solution)/shard_map/ppermute | solution.py:161
  22.4 3.2 %collective-permute-start.5 = (bf16[4,256,128]{2,1,0:T(8,128)(2,1)S(1)}, bf16[4,256,128]{2,1,0:T(8,128)(2,1)S(1)}, u32[]{:S(2)}, u32[]{:S(2)}) collective-permute-start(bf16[4,256,128]{2,1,0:T(8,128)(2,1)S(1)} %shard_map.65.refs_5_), channel_id=1, source_target_pairs={{0,0},{2,4},{4,2},{6,6},{1,1},{3,5},{5,3},{7,7},{8,8},{10,12},{12,... | collective-permute-start | bytes 786440 | tf_op jit(solution)/shard_map/ppermute | solution.py:161
  25.6 2.3 %collective-permute-done.6.refs_6_ = bf16[4,320,128]{2,1,0:T(8,128)(2,1)S(1)} collective-permute-done((bf16[4,320,128]{2,1,0:T(8,128)(2,1)S(1)}, bf16[4,320,128]{2,1,0:T(8,128)(2,1)S(1)}, u32[]{:S(2)}, u32[]{:S(2)}) %collective-permute-start.6) | collective-permute-done | bytes 327712 | tf_op jit(solution)/shard_map/ppermute | solution.py:161
  27.9 1.9 %collective-permute-done.7.refs_7_ = bf16[4,320,128]{2,1,0:T(8,128)(2,1)S(1)} collective-permute-done((bf16[4,320,128]{2,1,0:T(8,128)(2,1)S(1)}, bf16[4,320,128]{2,1,0:T(8,128)(2,1)S(1)}, u32[]{:S(2)}, u32[]{:S(2)}) %collective-permute-start.7) | collective-permute-done | bytes 327712 | tf_op jit(solution)/shard_map/ppermute | solution.py:161
  29.8 1.8 %shard_map.66 = (bf16[4,288,128]{2,1,0:T(8,128)(2,1)S(1)}, bf16[4,32,128]{2,1,0:T(8,128)(2,1)S(1)}, bf16[4,32,128]{2,1,0:T(8,128)(2,1)S(1)}) custom-call(f32[9,128]{1,0:T(8,128)S(1)} %get-tuple-element.30.refs_0_, f32[9,128]{1,0:T(8,128)S(1)} %get-tuple-element.29.refs_1_, f32[1,128]{1,0:T(1,128)S(1)} %get-tuple-element.26.refs_2_, ...), custom_call_target="tpu_custom_call" | custom-call | flops 1887436800 | bytes 1179648 | tf_op jit(solution)/shard_map/pallas_call | solution.py:127
  31.7 0.0 collective-permute-done.4.refs_6_
  31.7 1.0 %collective-permute-done.5.refs_7_ = bf16[4,256,128]{2,1,0:T(8,128)(2,1)S(1)} collective-permute-done((bf16[4,256,128]{2,1,0:T(8,128)(2,1)S(1)}, bf16[4,256,128]{2,1,0:T(8,128)(2,1)S(1)}, u32[]{:S(2)}, u32[]{:S(2)}) %collective-permute-start.5) | collective-permute-done | bytes 262176 | tf_op jit(solution)/shard_map/ppermute | solution.py:161
  32.7 1.7 %shard_map.67 = bf16[4,288,128]{2,1,0:T(8,128)(2,1)S(1)} custom-call(f32[9,128]{1,0:T(8,128)S(1)} %get-tuple-element.30.refs_0_, f32[9,128]{1,0:T(8,128)S(1)} %get-tuple-element.29.refs_1_, f32[1,128]{1,0:T(1,128)S(1)} %get-tuple-element.26.refs_2_, bf16[128,256]{1,0:T(8,128)(2,1)S(1)} %get-tuple-element.20.refs_3_, ...), custom_call_target="tpu_custom_call" | custom-call | flops 1887436800 | bytes 1179648 | tf_op jit(solution)/shard_map/pallas_call | solution.py:127
  34.4 0.9 %fusion.1 = bf16[1,4,576,128]{3,2,1,0:T(8,128)(2,1)} fusion(bf16[4,288,128]{2,1,0:T(8,128)(2,1)S(1)} %shard_map.67, bf16[4,288,128]{2,1,0:T(8,128)(2,1)S(1)} %get-tuple-element.16, bf16[4,32,128]{2,1,0:T(8,128)(2,1)S(1)} %slice.71), kind=kLoop, calls=%fused_computation.2 | loop fusion | flops 1769472 | bytes 1212416 | tf_op jit(solution)/shard_map/stack | solution.py:190
  (19 shorter events, 0.1 us)
Async XLA Ops:
  0.0 9.6 %copy-start.2 = (bf16[2,9,128]{2,0,1:T(2,128)(2,1)S(1)}, bf16[2,9,128]{2,0,1:T(2,128)(2,1)}, u32[]{:S(2)}) copy-start(bf16[2,9,128]{2,0,1:T(2,128)(2,1)} %param.8) | copy-start | bytes 13828
  0.0 9.7 %copy-start.3 = (bf16[2,9,128]{2,0,1:T(2,128)(2,1)S(1)}, bf16[2,9,128]{2,0,1:T(2,128)(2,1)}, u32[]{:S(2)}) copy-start(bf16[2,9,128]{2,0,1:T(2,128)(2,1)} %param.7) | copy-start | bytes 13828
  0.0 9.7 %copy-start = (bf16[2,256,128]{2,1,0:T(8,128)(2,1)S(1)}, bf16[2,256,128]{2,1,0:T(8,128)(2,1)}, u32[]{:S(2)}) copy-start(bf16[2,256,128]{2,1,0:T(8,128)(2,1)} %param.11) | copy-start | bytes 393220
  0.0 9.7 %copy-start.1 = (bf16[2,128,256]{2,1,0:T(8,128)(2,1)S(1)}, bf16[2,128,256]{2,1,0:T(8,128)(2,1)}, u32[]{:S(2)}) copy-start(bf16[2,128,256]{2,1,0:T(8,128)(2,1)} %param.10) | copy-start | bytes 393220
  1.1 8.7 %copy-start.4 = (f32[2,128]{1,0:T(2,128)S(1)}, f32[2,128]{1,0:T(2,128)}, u32[]{:S(2)}) copy-start(f32[2,128]{1,0:T(2,128)} %param.9) | copy-start | bytes 3076
  1.1 11.4 %collective-permute-start.2 = (bf16[4,352,128]{2,1,0:T(8,128)(2,1)S(1)}, bf16[4,352,128]{2,1,0:T(8,128)(2,1)S(1)}, u32[]{:S(2)}, u32[]{:S(2)}) collective-permute-start(bf16[4,352,128]{2,1,0:T(8,128)(2,1)S(1)} %slice.69.refs_5_.refs_8_), channel_id=1, source_target_pairs={{0,2},{2,0},{4,6},{6,4},{1,3},{3,1},{5,7},{7,5},{8,10},{10,8},{12,... | collective-permute-start | bytes 1081352 | tf_op jit(solution)/shard_map/ppermute | solution.py:161
  2.7 13.2 %collective-permute-start.3 = (bf16[4,352,128]{2,1,0:T(8,128)(2,1)S(1)}, bf16[4,352,128]{2,1,0:T(8,128)(2,1)S(1)}, u32[]{:S(2)}, u32[]{:S(2)}) collective-permute-start(bf16[4,352,128]{2,1,0:T(8,128)(2,1)S(1)} %slice.69.refs_5_.refs_8_), channel_id=1, source_target_pairs={{0,0},{2,4},{4,2},{6,6},{1,1},{3,5},{5,3},{7,7},{8,8},{10,12},{12,... | collective-permute-start | bytes 1081352 | tf_op jit(solution)/shard_map/ppermute | solution.py:161
  5.6 14.4 %collective-permute-start = (bf16[4,224,128]{2,1,0:T(8,128)(2,1)S(1)}, bf16[4,224,128]{2,1,0:T(8,128)(2,1)S(1)}, u32[]{:S(2)}, u32[]{:S(2)}) collective-permute-start(bf16[4,224,128]{2,1,0:T(8,128)(2,1)S(1)} %slice.68.refs_5_), channel_id=1, source_target_pairs={{0,2},{2,0},{4,6},{6,4},{1,3},{3,1},{5,7},{7,5},{8,10},{10,8},{12,... | collective-permute-start | bytes 688136 | tf_op jit(solution)/shard_map/ppermute | solution.py:161
  5.7 14.3 %collective-permute-start.1 = (bf16[4,224,128]{2,1,0:T(8,128)(2,1)S(1)}, bf16[4,224,128]{2,1,0:T(8,128)(2,1)S(1)}, u32[]{:S(2)}, u32[]{:S(2)}) collective-permute-start(bf16[4,224,128]{2,1,0:T(8,128)(2,1)S(1)} %slice.68.refs_5_), channel_id=1, source_target_pairs={{0,0},{2,4},{4,2},{6,6},{1,1},{3,5},{5,3},{7,7},{8,8},{10,12},{12,... | collective-permute-start | bytes 688136 | tf_op jit(solution)/shard_map/ppermute | solution.py:161
  18.0 9.9 %collective-permute-start.6 = (bf16[4,320,128]{2,1,0:T(8,128)(2,1)S(1)}, bf16[4,320,128]{2,1,0:T(8,128)(2,1)S(1)}, u32[]{:S(2)}, u32[]{:S(2)}) collective-permute-start(bf16[4,320,128]{2,1,0:T(8,128)(2,1)S(1)} %get-tuple-element.13.refs_5_.refs_8_), channel_id=1, source_target_pairs={{0,2},{2,0},{4,6},{6,4},{1,3},{3,1},{5,7},{7,5},{8,10},{10,8},{12,... | collective-permute-start | bytes 983048 | tf_op jit(solution)/shard_map/ppermute | solution.py:161
  18.1 11.8 %collective-permute-start.7 = (bf16[4,320,128]{2,1,0:T(8,128)(2,1)S(1)}, bf16[4,320,128]{2,1,0:T(8,128)(2,1)S(1)}, u32[]{:S(2)}, u32[]{:S(2)}) collective-permute-start(bf16[4,320,128]{2,1,0:T(8,128)(2,1)S(1)} %get-tuple-element.13.refs_5_.refs_8_), channel_id=1, source_target_pairs={{0,0},{2,4},{4,2},{6,6},{1,1},{3,5},{5,3},{7,7},{8,8},{10,12},{12,... | collective-permute-start | bytes 983048 | tf_op jit(solution)/shard_map/ppermute | solution.py:161
  21.6 10.1 %collective-permute-start.4 = (bf16[4,256,128]{2,1,0:T(8,128)(2,1)S(1)}, bf16[4,256,128]{2,1,0:T(8,128)(2,1)S(1)}, u32[]{:S(2)}, u32[]{:S(2)}) collective-permute-start(bf16[4,256,128]{2,1,0:T(8,128)(2,1)S(1)} %shard_map.65.refs_5_), channel_id=1, source_target_pairs={{0,2},{2,0},{4,6},{6,4},{1,3},{3,1},{5,7},{7,5},{8,10},{10,8},{12,... | collective-permute-start | bytes 786440 | tf_op jit(solution)/shard_map/ppermute | solution.py:161
  22.4 10.3 %collective-permute-start.5 = (bf16[4,256,128]{2,1,0:T(8,128)(2,1)S(1)}, bf16[4,256,128]{2,1,0:T(8,128)(2,1)S(1)}, u32[]{:S(2)}, u32[]{:S(2)}) collective-permute-start(bf16[4,256,128]{2,1,0:T(8,128)(2,1)S(1)} %shard_map.65.refs_5_), channel_id=1, source_target_pairs={{0,0},{2,4},{4,2},{6,6},{1,1},{3,5},{5,3},{7,7},{8,8},{10,12},{12,... | collective-permute-start | bytes 786440 | tf_op jit(solution)/shard_map/ppermute | solution.py:161

commit v5 on v4

--- a/solution.py
+++ b/solution.py
@@ -21,7 +21,7 @@
 
 def chunk_kernel(bands, first, last, width, *refs):
     refs = list(refs)
-    lat_w, lon_w, gain, w_in, w_out, own, even_swap, odd_swap = refs[:8]
+    lat_w, lon_w, gain, w_in, w_out, own, even_pair, odd_pair = refs[:8]
     refs = refs[8:]
     if not first:
         prev_own, prev_mix = refs[:2]
@@ -54,11 +54,13 @@
     def mix_tile(t, carry):
         at = pl.multiple_of(t * PAD, PAD)
         to = pl.multiple_of(start + t * PAD, PAD)
-        evens = [even_swap[r, pl.ds(at, PAD)] for r in range(REACH)]
-        odds = [odd_swap[r, pl.ds(at, PAD)] for r in range(REACH)]
-        none = jnp.zeros_like(evens[0])
-        above = [jnp.where(top, none, jnp.where(is_odd, e, o)) for e, o in zip(evens, odds)]
-        below = [jnp.where(bottom, none, jnp.where(is_odd, o, e)) for e, o in zip(evens, odds)]
+        above, below = [], []
+        for r in range(REACH):
+            here = (r, pl.ds(at, PAD))
+            up = jnp.where(is_odd, even_pair[(0,) + here], odd_pair[(0,) + here])
+            down = jnp.where(is_odd, odd_pair[(1,) + here], even_pair[(1,) + here])
+            above.append(jnp.where(top, jnp.zeros_like(up), up))
+            below.append(jnp.where(bottom, jnp.zeros_like(down), down))
         mine = [own[r, pl.ds(at, PAD)] for r in range(rows)]
         strip = [s.astype(jnp.float32) for s in above + mine + below]
         for r in range(rows):
@@ -107,11 +109,11 @@
 
 
 def layer_chunk(bands, weights, chunk, prev, first_chunk, first, last):
-    own, even_swap, odd_swap = chunk
+    own, even_pair, odd_pair = chunk
     rows, width, channels = own.shape
     made = width + (0 if first else PAD) + (0 if last else -PAD) + (PAD if last else 0) - (PAD if first else 0)
     window = made + 2 * PAD
-    args = list(weights) + [own, even_swap, odd_swap]
+    args = list(weights) + [own, even_pair, odd_pair]
     if not first:
         args += list(prev)
     if last and not first:
@@ -145,24 +147,28 @@
     return [(0, first), (first, total)]
 
 
-def swaps(bands, start):
-    to = list(range(bands))
+def pairs(bands, cores, start):
+    groups, alone = [], list(range(bands))
     for b in range(start, bands - 1, 2):
-        to[b], to[b + 1] = b + 1, b
-    return list(enumerate(to))
-
-
-def member_step(state, weights, bands):
+        groups += [[b * cores + m, (b + 1) * cores + m] for m in range(cores)]
+        alone.remove(b)
+        alone.remove(b + 1)
+    return groups + [[b * cores, b * cores + 1] for b in alone]
+
+
+def member_step(state, weights, bands, cores):
     rows, lons, _ = state.shape
-    even_pairs, odd_pairs = swaps(bands, 0), swaps(bands, 1)
+    both = [pairs(bands, cores, start) for start in (0, 1)]
     assert rows == REACH
     chunks = [state[:, lo:hi] for lo, hi in splits(lons)]
     for layer in range(LAYERS):
-        halos = [(lax.ppermute(own, "band", even_pairs), lax.ppermute(own, "band", odd_pairs)) for own in chunks]
+        halos = [
+            [lax.all_gather(own, ("band", "members"), axis_index_groups=groups) for groups in both] for own in chunks
+        ]
         made, prev, first_chunk = [], None, None
         for c, own in enumerate(chunks):
             first, last = c == 0, c == len(chunks) - 1
-            got = layer_chunk(bands, weights[layer], (own,) + halos[c], prev, first_chunk, first, last)
+            got = layer_chunk(bands, weights[layer], [own] + halos[c], prev, first_chunk, first, last)
             made.append(got[0])
             if not last:
                 prev = (own, got[1])
@@ -174,7 +180,8 @@
 
 
 def solution(mesh):
-    bands = mesh.shape["band"]
+    bands, cores = mesh.shape["band"], mesh.shape["members"]
+    assert cores == 2
 
     def shards(fields, lat_taps, lon_taps, gains, w_in, w_out):
         weights = [
@@ -187,7 +194,7 @@
             )
             for layer in range(LAYERS)
         ]
-        return jnp.stack([member_step(fields[m], weights, bands) for m in range(fields.shape[0])])
+        return jnp.stack([member_step(fields[m], weights, bands, cores) for m in range(fields.shape[0])])
 
     return jax.shard_map(
         shards,

time: 35.5 us -> 76.4 us (2.15)
  the two profiles are of different devices: /device:TPU:16 before, /device:TPU:8 now
where the time goes in v5:
time: 76.4 us; the launch traced here: 76 us
  blocking collectives  65.1 us (85%)
  Pallas kernels  7.09 us (9%)
  local copies, waits for them, and re-layouts  2.81 us (4%)
  other arithmetic  0.87 us (1%)
    all_gather x8, blocking collectives, member_step(): lax.all_gather(own, ('band', 'members'), axis_index_groups=groups)  65.1 us
    pallas_call x4, Pallas kernels, layer_chunk(): pl.pallas_call(functools.partial(chunk_kernel, bands, first, last, width)...  7.09 us
    slice x2, local copies, waits for them, and re-layouts, member_step(): chunks = [state[:, lo:hi] for lo, hi in splits(lons)]  1.97 us

profile of v5, /device:TPU:8, one launch (start us, length us, event | category | flops | bytes accessed | tf_op | source)
XLA Modules:
  0.0 76.0 jit_solution(17453284830714649101)
XLA Ops:
  0.0 1.0 %slice.69.refs_5_.refs_8_ = bf16[4,352,128]{2,1,0:T(8,128)(2,1)S(1)} slice(bf16[4,576,128]{2,1,0:T(8,128)(2,1)} %bitcast.47), slice={[0:4], [0:352], [0:128]} | slice | bytes 720896 | tf_op jit(solution)/shard_map/slice | solution.py:163
  1.0 10.8 %all-gather.2 = bf16[8,352,128]{2,1,0:T(8,128)(2,1)S(1)} all-gather(bf16[4,352,128]{2,1,0:T(8,128)(2,1)S(1)} %slice.69.refs_5_.refs_8_), channel_id=4, replica_groups={{0,2},{1,3},{4,6},{5,7},{8,10},{9,11},{12,14},{13,15},{16,18},{17,19},{..., dimensions={0}, use_global_device_ids=true | all-gather | bytes 1081344 | tf_op jit(solution)/shard_map/all_gather | solution.py:166
  11.8 0.0 copy-start.2
  11.8 0.0 copy-start
  11.9 0.0 copy-start.4
  11.9 10.1 %all-gather.3 = bf16[8,352,128]{2,1,0:T(8,128)(2,1)S(1)} all-gather(bf16[4,352,128]{2,1,0:T(8,128)(2,1)S(1)} %slice.69.refs_5_.refs_8_), channel_id=5, replica_groups={{2,4},{3,5},{0,1},{6,7},{10,12},{11,13},{8,9},{14,15},{18,20},{19,21},{..., dimensions={0}, use_global_device_ids=true | all-gather | bytes 1081344 | tf_op jit(solution)/shard_map/all_gather | solution.py:166
  22.0 0.0 copy-done.2
  22.0 0.0 copy-done.3
  22.0 0.0 copy-done
  22.0 0.0 copy-done.1
  22.1 0.0 copy-done.4
  22.1 2.0 %shard_map.64 = (bf16[4,320,128]{2,1,0:T(8,128)(2,1)S(1)}, bf16[4,32,128]{2,1,0:T(8,128)(2,1)S(1)}, bf16[4,32,128]{2,1,0:T(8,128)(2,1)S(1)}) custom-call(f32[9,128]{1,0:T(8,128)S(1)} %get-tuple-element.28.refs_0_, f32[9,128]{1,0:T(8,128)S(1)} %get-tuple-element.27.refs_1_, f32[1,128]{1,0:T(1,128)S(1)} %get-tuple-element.25.refs_2_, ...), custom_call_target="tpu_custom_call" | custom-call | flops 2097152000 | bytes 1310720 | tf_op jit(solution)/shard_map/pallas_call | solution.py:129
  24.1 8.3 %all-gather.6 = bf16[8,320,128]{2,1,0:T(8,128)(2,1)S(1)} all-gather(bf16[4,320,128]{2,1,0:T(8,128)(2,1)S(1)} %get-tuple-element.13.refs_5_.refs_8_), channel_id=8, replica_groups={{0,2},{1,3},{4,6},{5,7},{8,10},{9,11},{12,14},{13,15},{16,18},{17,19},{..., dimensions={0}, use_global_device_ids=true | all-gather | bytes 983040 | tf_op jit(solution)/shard_map/all_gather | solution.py:166
  32.5 7.7 %all-gather.7 = bf16[8,320,128]{2,1,0:T(8,128)(2,1)S(1)} all-gather(bf16[4,320,128]{2,1,0:T(8,128)(2,1)S(1)} %get-tuple-element.13.refs_5_.refs_8_), channel_id=9, replica_groups={{2,4},{3,5},{0,1},{6,7},{10,12},{11,13},{8,9},{14,15},{18,20},{19,21},{..., dimensions={0}, use_global_device_ids=true | all-gather | bytes 983040 | tf_op jit(solution)/shard_map/all_gather | solution.py:166
  40.2 1.8 %shard_map.66 = (bf16[4,288,128]{2,1,0:T(8,128)(2,1)S(1)}, bf16[4,32,128]{2,1,0:T(8,128)(2,1)S(1)}, bf16[4,32,128]{2,1,0:T(8,128)(2,1)S(1)}) custom-call(f32[9,128]{1,0:T(8,128)S(1)} %get-tuple-element.30.refs_0_, f32[9,128]{1,0:T(8,128)S(1)} %get-tuple-element.29.refs_1_, f32[1,128]{1,0:T(1,128)S(1)} %get-tuple-element.26.refs_2_, ...), custom_call_target="tpu_custom_call" | custom-call | flops 1887436800 | bytes 1179648 | tf_op jit(solution)/shard_map/pallas_call | solution.py:129
  42.0 1.0 %slice.68.refs_5_ = bf16[4,224,128]{2,1,0:T(8,128)(2,1)S(1)} slice(bf16[4,576,128]{2,1,0:T(8,128)(2,1)} %bitcast.48), slice={[0:4], [352:576], [0:128]} | slice | bytes 458752 | tf_op jit(solution)/shard_map/slice | solution.py:163
  43.0 6.7 %all-gather.1 = bf16[8,224,128]{2,1,0:T(8,128)(2,1)S(1)} all-gather(bf16[4,224,128]{2,1,0:T(8,128)(2,1)S(1)} %slice.68.refs_5_), channel_id=3, replica_groups={{2,4},{3,5},{0,1},{6,7},{10,12},{11,13},{8,9},{14,15},{18,20},{19,21},{..., dimensions={0}, use_global_device_ids=true | all-gather | bytes 688128 | tf_op jit(solution)/shard_map/all_gather | solution.py:166
  49.7 7.4 %all-gather = bf16[8,224,128]{2,1,0:T(8,128)(2,1)S(1)} all-gather(bf16[4,224,128]{2,1,0:T(8,128)(2,1)S(1)} %slice.68.refs_5_), channel_id=2, replica_groups={{0,2},{1,3},{4,6},{5,7},{8,10},{9,11},{12,14},{13,15},{16,18},{17,19},{..., dimensions={0}, use_global_device_ids=true | all-gather | bytes 688128 | tf_op jit(solution)/shard_map/all_gather | solution.py:166
  57.1 0.8 %slice.70.refs_10_ = bf16[4,32,128]{2,1,0:T(8,128)(2,1)S(1)} slice(bf16[4,576,128]{2,1,0:T(8,128)(2,1)} %bitcast.49), slice={[0:4], [0:32], [0:128]} | slice | bytes 65536 | tf_op jit(solution)/shard_map/slice | solution.py:176
  57.8 1.5 %shard_map.65.refs_5_ = bf16[4,256,128]{2,1,0:T(8,128)(2,1)S(1)} custom-call(f32[9,128]{1,0:T(8,128)S(1)} %get-tuple-element.28.refs_0_, f32[9,128]{1,0:T(8,128)S(1)} %get-tuple-element.27.refs_1_, f32[1,128]{1,0:T(1,128)S(1)} %get-tuple-element.25.refs_2_, bf16[128,256]{1,0:T(8,128)(2,1)S(1)} %get-tuple-element.19.refs_3_, ...), custom_call_target="tpu_custom_call" | custom-call | flops 1677721600 | bytes 1048576 | tf_op jit(solution)/shard_map/pallas_call | solution.py:129
  59.4 7.0 %all-gather.4 = bf16[8,256,128]{2,1,0:T(8,128)(2,1)S(1)} all-gather(bf16[4,256,128]{2,1,0:T(8,128)(2,1)S(1)} %shard_map.65.refs_5_), channel_id=6, replica_groups={{0,2},{1,3},{4,6},{5,7},{8,10},{9,11},{12,14},{13,15},{16,18},{17,19},{..., dimensions={0}, use_global_device_ids=true | all-gather | bytes 786432 | tf_op jit(solution)/shard_map/all_gather | solution.py:166
  66.4 7.0 %all-gather.5 = bf16[8,256,128]{2,1,0:T(8,128)(2,1)S(1)} all-gather(bf16[4,256,128]{2,1,0:T(8,128)(2,1)S(1)} %shard_map.65.refs_5_), channel_id=7, replica_groups={{2,4},{3,5},{0,1},{6,7},{10,12},{11,13},{8,9},{14,15},{18,20},{19,21},{..., dimensions={0}, use_global_device_ids=true | all-gather | bytes 786432 | tf_op jit(solution)/shard_map/all_gather | solution.py:166
  73.5 1.7 %shard_map.67 = bf16[4,288,128]{2,1,0:T(8,128)(2,1)S(1)} custom-call(f32[9,128]{1,0:T(8,128)S(1)} %get-tuple-element.30.refs_0_, f32[9,128]{1,0:T(8,128)S(1)} %get-tuple-element.29.refs_1_, f32[1,128]{1,0:T(1,128)S(1)} %get-tuple-element.26.refs_2_, bf16[128,256]{1,0:T(8,128)(2,1)S(1)} %get-tuple-element.20.refs_3_, ...), custom_call_target="tpu_custom_call" | custom-call | flops 1887436800 | bytes 1179648 | tf_op jit(solution)/shard_map/pallas_call | solution.py:129
  75.2 0.9 %fusion.1 = bf16[1,4,576,128]{3,2,1,0:T(8,128)(2,1)} fusion(bf16[4,288,128]{2,1,0:T(8,128)(2,1)S(1)} %shard_map.67, bf16[4,288,128]{2,1,0:T(8,128)(2,1)S(1)} %get-tuple-element.16, bf16[4,32,128]{2,1,0:T(8,128)(2,1)S(1)} %slice.71), kind=kLoop, calls=%fused_computation.2 | loop fusion | flops 1769472 | bytes 1212416 | tf_op jit(solution)/shard_map/stack | solution.py:197
  (11 shorter events, 0.1 us)
Async XLA Ops:
  11.8 10.1 %copy-start.2 = (bf16[2,9,128]{2,0,1:T(2,128)(2,1)S(1)}, bf16[2,9,128]{2,0,1:T(2,128)(2,1)}, u32[]{:S(2)}) copy-start(bf16[2,9,128]{2,0,1:T(2,128)(2,1)} %param.8) | copy-start | bytes 13828
  11.8 10.1 %copy-start.3 = (bf16[2,9,128]{2,0,1:T(2,128)(2,1)S(1)}, bf16[2,9,128]{2,0,1:T(2,128)(2,1)}, u32[]{:S(2)}) copy-start(bf16[2,9,128]{2,0,1:T(2,128)(2,1)} %param.7) | copy-start | bytes 13828
  11.8 10.2 %copy-start = (bf16[2,256,128]{2,1,0:T(8,128)(2,1)S(1)}, bf16[2,256,128]{2,1,0:T(8,128)(2,1)}, u32[]{:S(2)}) copy-start(bf16[2,256,128]{2,1,0:T(8,128)(2,1)} %param.11) | copy-start | bytes 393220
  11.8 10.2 %copy-start.1 = (bf16[2,128,256]{2,1,0:T(8,128)(2,1)S(1)}, bf16[2,128,256]{2,1,0:T(8,128)(2,1)}, u32[]{:S(2)}) copy-start(bf16[2,128,256]{2,1,0:T(8,128)(2,1)} %param.10) | copy-start | bytes 393220
  11.9 10.2 %copy-start.4 = (f32[2,128]{1,0:T(2,128)S(1)}, f32[2,128]{1,0:T(2,128)}, u32[]{:S(2)}) copy-start(f32[2,128]{1,0:T(2,128)} %param.9) | copy-start | bytes 3076

commit v6 on v4

v6 whole, which is shorter than its diff:
```python
import functools

import jax
import jax.numpy as jnp
from jax import lax
from jax.experimental import pallas as pl
from jax.experimental.pallas import tpu as pltpu
from jax.sharding import PartitionSpec as P

DLON = 3
LAYERS = 2
TAPS = 9
REACH = TAPS // 2
PAD = 16
TILE = 32
ERFC_POWER = (
    -1.000037622280944,
    -1.1507878529643598,
    -0.459992437236149,
    -0.051827384082804726,
    0.007084557514732341,
    -0.00047330932043343645,
)


def gelu(x):
    size = jnp.abs(x)
    power = ERFC_POWER[-1] * size + ERFC_POWER[-2]
    for c in ERFC_POWER[-3::-1]:
        power = power * size + c
    return jnp.maximum(x, 0.0) - size * jnp.exp2(power)


def own_kernel(ranges, lat_w, state, *outs):
    rows, channels = state.shape[0], state.shape[2]
    lat_tap = [jnp.broadcast_to(lat_w[k : k + 1], (PAD, channels)) for k in range(TAPS)]
    for (lo, hi), sums in zip(ranges, outs[: len(ranges)]):

        def tile(t, carry):
            at = pl.multiple_of(t * PAD, PAD)
            here = pl.multiple_of(lo + t * PAD, PAD)
            own = [state[r, pl.ds(here, PAD)].astype(jnp.float32) for r in range(rows)]
            for r in range(rows):
                total = own[0] * lat_tap[REACH - r]
                for k in range(1, rows):
                    total = total + own[k] * lat_tap[REACH - r + k]
                sums[r, pl.ds(at, PAD)] = total
            return carry

        lax.fori_loop(0, (hi - lo) // PAD, tile, 0)
    for (lo, hi), copy in zip(ranges[1:], outs[len(ranges) :]):
        copy[...] = state[:, lo:hi]


def own_share(lat_w, state, ranges):
    rows, _, channels = state.shape
    shapes = [jax.ShapeDtypeStruct((rows, hi - lo, channels), jnp.float32) for lo, hi in ranges]
    shapes += [jax.ShapeDtypeStruct((rows, hi - lo, channels), jnp.bfloat16) for lo, hi in ranges[1:]]
    cells = rows * state.shape[1]
    got = pl.pallas_call(
        functools.partial(own_kernel, ranges),
        out_shape=shapes,
        in_specs=[pl.BlockSpec(memory_space=pltpu.VMEM)] * 2,
        out_specs=[pl.BlockSpec(memory_space=pltpu.VMEM)] * len(shapes),
        compiler_params=pltpu.CompilerParams(vmem_limit_bytes=16 * 2**20),
        cost_estimate=pl.CostEstimate(
            flops=3200 * cells * channels, bytes_accessed=8 * cells * channels, transcendentals=0
        ),
    )(lat_w, state)
    return list(got[: len(ranges)]), list(got[len(ranges) :])


def chunk_kernel(bands, first, last, width, place, *refs):
    refs = list(refs)
    lat_w, lon_w, gain, w_in, w_out, own, sums, even_swap, odd_swap = refs[:9]
    refs = refs[9:]
    if not first:
        prev_own, prev_mix = refs[:2]
        refs = refs[2:]
    if last and not first:
        first_own, first_mix = refs[:2]
        refs = refs[2:]
    if place is not None and not first:
        refs.pop(0)
    out = refs.pop(0)
    if not last:
        tail = refs.pop(0)
    if first and not last:
        head = refs.pop(0)
    mix, state = refs[:2]
    whole = out
    if place is not None:
        out, sems = refs[2:]
    rows = own.shape[0]
    channels = own.shape[2]
    start = 0 if first else 2 * PAD

    if not first:
        mix[:, : 2 * PAD] = prev_mix[...].astype(jnp.float32)
        state[:, : 2 * PAD] = prev_own[:, prev_own.shape[1] - 2 * PAD :]
    if last and not first:
        mix[:, start + width :] = first_mix[...].astype(jnp.float32)
        state[:, start + width :] = first_own[:, : 2 * PAD]

    band = lax.axis_index("band")
    is_odd = lax.rem(band, 2) == 1
    lat_tap = [jnp.broadcast_to(lat_w[k : k + 1], (PAD, channels)) for k in range(TAPS)]

    def mix_tile(t, carry):
        at = pl.multiple_of(t * PAD, PAD)
        to = pl.multiple_of(start + t * PAD, PAD)
        evens = [even_swap[r, pl.ds(at, PAD)] for r in range(REACH)]
        odds = [odd_swap[r, pl.ds(at, PAD)] for r in range(REACH)]
        above = [jnp.where(is_odd, e, o) for e, o in zip(evens, odds)]
        below = [jnp.where(is_odd, o, e) for e, o in zip(evens, odds)]
        above = [s.astype(jnp.float32) for s in above]
        below = [s.astype(jnp.float32) for s in below]
        for r in range(rows):
            total = sums[r, pl.ds(at, PAD)]
            for k in range(REACH - r):
                total = total + above[r + k] * lat_tap[k]
            for k in range(TAPS - 1 - r, TAPS):
                total = total + below[r + k - TAPS + 1] * lat_tap[k]
            mix[r, pl.ds(to, PAD)] = total.astype(jnp.bfloat16).astype(jnp.float32)
            state[r, pl.ds(to, PAD)] = own[r, pl.ds(at, PAD)]
        return carry

    lax.fori_loop(0, width // PAD, mix_tile, 0)

    if not last:
        tail[...] = mix[:, start + width - 2 * PAD : start + width].astype(jnp.bfloat16)
    if first and not last:
        head[...] = mix[:, : 2 * PAD].astype(jnp.bfloat16)
    if first and last:
        mix[:, width:] = mix[:, : 2 * PAD]
        state[:, width:] = state[:, : 2 * PAD]

    lon_tap = [lon_w[k : k + 1] for k in range(TAPS)]
    scale = gain[...]
    made, total = out.shape[1], whole.shape[1]

    def rest(at, tile):
        parts = []
        for r in range(rows):
            lon = mix[r, pl.ds(at + PAD - DLON * REACH, tile)] * lon_tap[0]
            for k in range(1, TAPS):
                lon = lon + mix[r, pl.ds(at + PAD + DLON * (k - REACH), tile)] * lon_tap[k]
            parts.append(lon)
        lon = jnp.concatenate(parts, axis=0)
        mean = jnp.mean(lon, axis=-1, keepdims=True)
        centred = lon - mean
        var = jnp.mean(centred * centred, axis=-1, keepdims=True)
        normed = (centred * lax.rsqrt(var + 1e-06) * scale).astype(jnp.bfloat16)
        hidden = jnp.dot(normed, w_in[...], preferred_element_type=jnp.float32)
        hidden = gelu(hidden).astype(jnp.bfloat16)
        delta = jnp.dot(hidden, w_out[...], preferred_element_type=jnp.float32)
        for r in range(rows):
            new = state[r, pl.ds(at + PAD, tile)].astype(jnp.float32) + delta[r * tile : (r + 1) * tile]
            out[r, pl.ds(at, tile)] = new.astype(jnp.bfloat16)

    copies = []
    for at, tile in tiles(made):
        rest(at, tile)
        if place is not None:
            to = (place + at) % total
            copies.append(
                pltpu.make_async_copy(out.at[:, at : at + tile], whole.at[:, to : to + tile], sems.at[len(copies)])
            )
            copies[-1].start()
    for copy in copies:
        copy.wait()


def tiles(made):
    return [(at, min(TILE, made - at)) for at in range(0, made, TILE)]


def layer_chunk(bands, weights, chunk, prev, first_chunk, first, last, place=None, whole=None):
    own = chunk[0]
    rows, width, channels = own.shape
    made = width + (0 if first else PAD) + (0 if last else -PAD) + (PAD if last else 0) - (PAD if first else 0)
    window = made + 2 * PAD
    args = list(weights) + list(chunk)
    if not first:
        args += list(prev)
    if last and not first:
        args += list(first_chunk)
    specs = [pl.BlockSpec(memory_space=pltpu.VMEM)] * len(args)
    strip = jax.ShapeDtypeStruct((rows, 2 * PAD, channels), jnp.bfloat16)
    outs = [jax.ShapeDtypeStruct((rows, made, channels), jnp.bfloat16)]
    out_specs = [pl.BlockSpec(memory_space=pltpu.VMEM)]
    scratch = [
        pltpu.VMEM((rows, window, channels), jnp.float32),
        pltpu.VMEM((rows, window, channels), jnp.bfloat16),
    ]
    aliases = {}
    if place is not None:
        scratch += [pltpu.VMEM(outs[0].shape, jnp.bfloat16), pltpu.SemaphoreType.DMA((len(tiles(made)),))]
        outs = [jax.ShapeDtypeStruct((rows, whole if first else whole.shape[1], channels), jnp.bfloat16)]
        out_specs = [pl.BlockSpec(memory_space=pltpu.HBM)]
        if not first:
            aliases = {len(args): 0}
            args.append(whole)
            specs += out_specs
    if not last:
        outs.append(strip)
    if first and not last:
        outs.append(strip)
    out_specs += [pl.BlockSpec(memory_space=pltpu.VMEM)] * (len(outs) - 1)
    cells = rows * made
    hidden = weights[3].shape[1]
    return pl.pallas_call(
        functools.partial(chunk_kernel, bands, first, last, width, place),
        out_shape=outs,
        in_specs=specs,
        out_specs=out_specs,
        scratch_shapes=scratch,
        input_output_aliases=aliases,
        compiler_params=pltpu.CompilerParams(vmem_limit_bytes=24 * 2**20),
        cost_estimate=pl.CostEstimate(
            flops=50 * cells * channels * hidden, bytes_accessed=8 * cells * channels, transcendentals=cells * hidden
        ),
    )(*args)


def splits(total):
    first = PAD * ((total // PAD + 4 * LAYERS) // 2)
    return [(0, first), (first, total)]


def swaps(bands, start):
    return [pair for b in range(start, bands - 1, 2) for pair in ((b, b + 1), (b + 1, b))]


def member_step(state, weights, bands):
    rows, lons, _ = state.shape
    assert rows == REACH
    even_pairs, odd_pairs = swaps(bands, 0), swaps(bands, 1)
    ranges = splits(lons)
    sums, later = own_share(weights[0][0], state, ranges)
    chunks = [state[:, : ranges[0][1]]] + later
    whole, place = lons, LAYERS * PAD
    for layer in range(LAYERS):
        halos = [(lax.ppermute(own, "band", even_pairs), lax.ppermute(own, "band", odd_pairs)) for own in chunks]
        if layer > 0:
            sums = [own_share(weights[layer][0], own, [(0, own.shape[1])])[0][0] for own in chunks]
        final = layer == LAYERS - 1
        made, prev, first_chunk = [], None, None
        for c, own in enumerate(chunks):
            first, last = c == 0, c == len(chunks) - 1
            where = (place, whole) if final else ()
            got = layer_chunk(bands, weights[layer], (own, sums[c]) + halos[c], prev, first_chunk, first, last, *where)
            made.append(got[0])
            if final:
                whole = got[0]
                place += own.shape[1] - (2 * PAD if first else 0)
            if not last:
                prev = (own, got[1])
            if first and not last:
                first_chunk = (own[:, : 2 * PAD], got[2])
        chunks = made
    return whole


def solution(mesh):
    bands = mesh.shape["band"]

    def shards(fields, lat_taps, lon_taps, gains, w_in, w_out):
        weights = [
            (
                lat_taps[layer].astype(jnp.float32),
                lon_taps[layer].astype(jnp.float32),
                gains[layer : layer + 1],
                w_in[layer],
                w_out[layer],
            )
            for layer in range(LAYERS)
        ]
        return jnp.concatenate([member_step(fields[m], weights, bands)[None] for m in range(fields.shape[0])])

    return jax.shard_map(
        shards,
        mesh=mesh,
        in_specs=(P(("members", "section"), "band", None, None), P(), P(), P(), P(), P()),
        out_specs=P(("members", "section"), "band", None, None),
        check_vma=False,
    )
```

time: 35.5 us -> 35.5 us (level)
  the two profiles are of different devices: /device:TPU:16 before, /device:TPU:18 now
where the time goes in v6:
time: 35.5 us; the launch traced here: 35.3 us
  starting transfers between devices  13.5 us (38%)
  Pallas kernels  10.1 us (28%)
  waiting for transfers between devices  8.91 us (25%)
  local copies, waits for them, and re-layouts  2.49 us (7%)
    ppermute x4, starting transfers between devices, member_step(): lax.ppermute(own, 'band', odd_pairs)  10.9 us
    pallas_call x4, Pallas kernels, layer_chunk(): pl.pallas_call(functools.partial(chunk_kernel, bands, first, last, width,...  9.01 us
    ppermute x4, waiting for transfers between devices, member_step(): lax.ppermute(own, 'band', odd_pairs)  5.54 us
    ppermute x4, waiting for transfers between devices, member_step(): lax.ppermute(own, 'band', even_pairs)  3.37 us
    ppermute x4, starting transfers between devices, member_step(): lax.ppermute(own, 'band', even_pairs)  2.61 us
    unnamed x12, local copies, waits for them, and re-layouts  1.35 us
    pallas_call x3, Pallas kernels, own_share(): pl.pallas_call(functools.partial(own_kernel, ranges), out_shape=shapes, i...  1.1 us
    slice x1, local copies, waits for them, and re-layouts, member_step(): chunks = [state[:, :ranges[0][1]]] + later  1.08 us
  transfers between devices with their start and end apart: 8, of which 5 were waited for; matrix products, arithmetic and copies ran while one was open for 0% of the time, Pallas kernels for 21%

profile of v6, /device:TPU:18, one launch (start us, length us, event | category | flops | bytes accessed | tf_op | source)
XLA Modules:
  0.0 35.3 jit_solution(12761160590854224518)
XLA Ops:
  0.0 1.1 %slice.53.refs_5_.refs_9_ = bf16[4,352,128]{2,1,0:T(8,128)(2,1)S(1)} slice(bf16[4,576,128]{2,1,0:T(8,128)(2,1)} %bitcast.30), slice={[0:4], [0:352], [0:128]} | slice | bytes 720896 | tf_op jit(solution)/shard_map/slice | solution.py:241
  1.1 1.6 %collective-permute-start.2 = (bf16[4,352,128]{2,1,0:T(8,128)(2,1)S(1)}, bf16[4,352,128]{2,1,0:T(8,128)(2,1)S(1)}, u32[]{:S(2)}, u32[]{:S(2)}) collective-permute-start(bf16[4,352,128]{2,1,0:T(8,128)(2,1)S(1)} %slice.53.refs_5_.refs_9_), channel_id=1, source_target_pairs={{0,2},{2,0},{4,6},{6,4},{1,3},{3,1},{5,7},{7,5},{8,10},{10,8},{12,... | collective-permute-start | bytes 1081352 | tf_op jit(solution)/shard_map/ppermute | solution.py:244
  2.7 1.9 %collective-permute-start.3 = (bf16[4,352,128]{2,1,0:T(8,128)(2,1)S(1)}, bf16[4,352,128]{2,1,0:T(8,128)(2,1)S(1)}, u32[]{:S(2)}, u32[]{:S(2)}) collective-permute-start(bf16[4,352,128]{2,1,0:T(8,128)(2,1)S(1)} %slice.53.refs_5_.refs_9_), channel_id=1, source_target_pairs={{2,4},{4,2},{3,5},{5,3},{10,12},{12,10},{11,13},{13,11},{18,20},{2... | collective-permute-start | bytes 1081352 | tf_op jit(solution)/shard_map/ppermute | solution.py:244
  4.7 0.6 %shard_map.64 = (f32[4,352,128]{2,1,0:T(8,128)S(1)}, f32[4,224,128]{2,1,0:T(8,128)S(1)}, bf16[4,224,128]{2,1,0:T(8,128)(2,1)S(1)}) custom-call(f32[9,128]{1,0:T(8,128)S(1)} %fusion.1.lat_w.refs_0_, bf16[4,576,128]{2,1,0:T(8,128)(2,1)S(1)} %bitcast.31), custom_call_target="tpu_custom_call" | custom-call | flops 943718400 | bytes 2359296 | tf_op jit(solution)/shard_map/pallas_call | solution.py:60
  5.3 0.0 copy-start.2
  5.3 0.1 collective-permute-start
  5.4 3.9 %collective-permute-start.1 = (bf16[4,224,128]{2,1,0:T(8,128)(2,1)S(1)}, bf16[4,224,128]{2,1,0:T(8,128)(2,1)S(1)}, u32[]{:S(2)}, u32[]{:S(2)}) collective-permute-start(bf16[4,224,128]{2,1,0:T(8,128)(2,1)S(1)} %get-tuple-element.14.refs_5_), channel_id=1, source_target_pairs={{2,4},{4,2},{3,5},{5,3},{10,12},{12,10},{11,13},{13,11},{18,20},{2... | collective-permute-start | bytes 688136 | tf_op jit(solution)/shard_map/ppermute | solution.py:244
  9.3 0.7 %copy-done.4 = bf16[2,9,128]{2,0,1:T(2,128)(2,1)S(1)} copy-done((bf16[2,9,128]{2,0,1:T(2,128)(2,1)S(1)}, bf16[2,9,128]{2,0,1:T(2,128)(2,1)}, u32[]{:S(2)}) %copy-start.4) | copy-done | bytes 4632
  10.0 0.7 %copy-done.5 = f32[2,128]{1,0:T(2,128)S(1)} copy-done((f32[2,128]{1,0:T(2,128)S(1)}, f32[2,128]{1,0:T(2,128)}, u32[]{:S(2)}) %copy-start.5) | copy-done | bytes 1048
  10.7 1.7 %collective-permute-done.2.refs_7_ = bf16[4,352,128]{2,1,0:T(8,128)(2,1)S(1)} collective-permute-done((bf16[4,352,128]{2,1,0:T(8,128)(2,1)S(1)}, bf16[4,352,128]{2,1,0:T(8,128)(2,1)S(1)}, u32[]{:S(2)}, u32[]{:S(2)}) %collective-permute-start.2) | collective-permute-done | bytes 360480 | tf_op jit(solution)/shard_map/ppermute | solution.py:244
  12.5 3.5 %collective-permute-done.3.refs_8_ = bf16[4,352,128]{2,1,0:T(8,128)(2,1)S(1)} collective-permute-done((bf16[4,352,128]{2,1,0:T(8,128)(2,1)S(1)}, bf16[4,352,128]{2,1,0:T(8,128)(2,1)S(1)}, u32[]{:S(2)}, u32[]{:S(2)}) %collective-permute-start.3) | collective-permute-done | bytes 360480 | tf_op jit(solution)/shard_map/ppermute | solution.py:244
  16.0 2.1 %shard_map.65 = (bf16[4,320,128]{2,1,0:T(8,128)(2,1)S(1)}, bf16[4,32,128]{2,1,0:T(8,128)(2,1)S(1)}, bf16[4,32,128]{2,1,0:T(8,128)(2,1)S(1)}) custom-call(f32[9,128]{1,0:T(8,128)S(1)} %fusion.1.lat_w.refs_0_, f32[9,128]{1,0:T(8,128)S(1)} %fusion.refs_1_, f32[1,128]{1,0:T(1,128)S(1)} %get-tuple-element.31.refs_2_, ...), custom_call_target="tpu_custom_call" | custom-call | flops 2097152000 | bytes 1310720 | tf_op jit(solution)/shard_map/pallas_call | solution.py:212
  18.1 0.1 collective-permute-start.6
  18.2 1.9 %collective-permute-start.7 = (bf16[4,320,128]{2,1,0:T(8,128)(2,1)S(1)}, bf16[4,320,128]{2,1,0:T(8,128)(2,1)S(1)}, u32[]{:S(2)}, u32[]{:S(2)}) collective-permute-start(bf16[4,320,128]{2,1,0:T(8,128)(2,1)S(1)} %get-tuple-element.19.state.refs_5_.refs_9_), channel_id=1, source_target_pairs={{2,4},{4,2},{3,5},{5,3},{10,12},{12,10},{11,13},{13,11},{18,20},{2... | collective-permute-start | bytes 983048 | tf_op jit(solution)/shard_map/ppermute | solution.py:244
  20.1 1.7 %shard_map.66.state.refs_5_ = bf16[4,256,128]{2,1,0:T(8,128)(2,1)S(1)} custom-call(f32[9,128]{1,0:T(8,128)S(1)} %fusion.1.lat_w.refs_0_, f32[9,128]{1,0:T(8,128)S(1)} %fusion.refs_1_, f32[1,128]{1,0:T(1,128)S(1)} %get-tuple-element.31.refs_2_, bf16[128,256]{1,0:T(8,128)(2,1)S(1)} %get-tuple-element.25.refs_3_, ...), custom_call_target="tpu_custom_call" | custom-call | flops 1677721600 | bytes 1048576 | tf_op jit(solution)/shard_map/pallas_call | solution.py:212
  21.8 0.8 %collective-permute-start.4 = (bf16[4,256,128]{2,1,0:T(8,128)(2,1)S(1)}, bf16[4,256,128]{2,1,0:T(8,128)(2,1)S(1)}, u32[]{:S(2)}, u32[]{:S(2)}) collective-permute-start(bf16[4,256,128]{2,1,0:T(8,128)(2,1)S(1)} %shard_map.66.state.refs_5_), channel_id=1, source_target_pairs={{0,2},{2,0},{4,6},{6,4},{1,3},{3,1},{5,7},{7,5},{8,10},{10,8},{12,... | collective-permute-start | bytes 786440 | tf_op jit(solution)/shard_map/ppermute | solution.py:244
  22.6 3.2 %collective-permute-start.5 = (bf16[4,256,128]{2,1,0:T(8,128)(2,1)S(1)}, bf16[4,256,128]{2,1,0:T(8,128)(2,1)S(1)}, u32[]{:S(2)}, u32[]{:S(2)}) collective-permute-start(bf16[4,256,128]{2,1,0:T(8,128)(2,1)S(1)} %shard_map.66.state.refs_5_), channel_id=1, source_target_pairs={{2,4},{4,2},{3,5},{5,3},{10,12},{12,10},{11,13},{13,11},{18,20},{2... | collective-permute-start | bytes 786440 | tf_op jit(solution)/shard_map/ppermute | solution.py:244
  25.8 0.2 shard_map.67.refs_6_
  26.1 0.3 shard_map.68.refs_6_
  26.4 1.6 %collective-permute-done.6.refs_7_ = bf16[4,320,128]{2,1,0:T(8,128)(2,1)S(1)} collective-permute-done((bf16[4,320,128]{2,1,0:T(8,128)(2,1)S(1)}, bf16[4,320,128]{2,1,0:T(8,128)(2,1)S(1)}, u32[]{:S(2)}, u32[]{:S(2)}) %collective-permute-start.6) | collective-permute-done | bytes 327712 | tf_op jit(solution)/shard_map/ppermute | solution.py:244
  28.0 1.9 %collective-permute-done.7.refs_8_ = bf16[4,320,128]{2,1,0:T(8,128)(2,1)S(1)} collective-permute-done((bf16[4,320,128]{2,1,0:T(8,128)(2,1)S(1)}, bf16[4,320,128]{2,1,0:T(8,128)(2,1)S(1)}, u32[]{:S(2)}, u32[]{:S(2)}) %collective-permute-start.7) | collective-permute-done | bytes 327712 | tf_op jit(solution)/shard_map/ppermute | solution.py:244
  29.9 2.7 %shard_map.69 = (bf16[4,576,128]{2,1,0:T(8,128)(2,1)}, bf16[4,32,128]{2,1,0:T(8,128)(2,1)S(1)}, bf16[4,32,128]{2,1,0:T(8,128)(2,1)S(1)}) custom-call(f32[9,128]{1,0:T(8,128)S(1)} %get-tuple-element.34.lat_w.refs_0_, f32[9,128]{1,0:T(8,128)S(1)} %get-tuple-element.33.refs_1_, f32[1,128]{1,0:T(1,128)S(1)} %get-tuple-element.32.refs_2_, ...), custom_call_target="tpu_custom_call" | custom-call | flops 1887436800 | bytes 1179648 | tf_op jit(solution)/shard_map/pallas_call | solution.py:212
  32.6 0.1 collective-permute-done.5.refs_8_
  32.7 2.6 %shard_map.70 = bf16[4,576,128]{2,1,0:T(8,128)(2,1)} custom-call(f32[9,128]{1,0:T(8,128)S(1)} %get-tuple-element.34.lat_w.refs_0_, f32[9,128]{1,0:T(8,128)S(1)} %get-tuple-element.33.refs_1_, f32[1,128]{1,0:T(1,128)S(1)} %get-tuple-element.32.refs_2_, bf16[128,256]{1,0:T(8,128)(2,1)S(1)} %get-tuple-element.26.refs_3_, ...), custom_call_target="tpu_custom_call", output_to_operand_aliasing={{}: (13, {})} | custom-call | flops 1887436800 | bytes 1179648 | tf_op jit(solution)/shard_map/pallas_call | solution.py:212
  (22 shorter events, 0.1 us)
Async XLA Ops:
  0.0 4.7 %copy-start = (bf16[1,4,576,128]{3,2,1,0:T(8,128)(2,1)S(1)}, bf16[1,4,576,128]{3,2,1,0:T(8,128)(2,1)}, u32[]{:S(2)}) copy-start(bf16[1,4,576,128]{3,2,1,0:T(8,128)(2,1)} %param.6) | copy-start | bytes 1769476
  0.0 4.7 %copy-start.3 = (bf16[2,9,128]{2,0,1:T(2,128)(2,1)S(1)}, bf16[2,9,128]{2,0,1:T(2,128)(2,1)}, u32[]{:S(2)}) copy-start(bf16[2,9,128]{2,0,1:T(2,128)(2,1)} %param.7) | copy-start | bytes 13828
  1.1 11.4 %collective-permute-start.2 = (bf16[4,352,128]{2,1,0:T(8,128)(2,1)S(1)}, bf16[4,352,128]{2,1,0:T(8,128)(2,1)S(1)}, u32[]{:S(2)}, u32[]{:S(2)}) collective-permute-start(bf16[4,352,128]{2,1,0:T(8,128)(2,1)S(1)} %slice.53.refs_5_.refs_9_), channel_id=1, source_target_pairs={{0,2},{2,0},{4,6},{6,4},{1,3},{3,1},{5,7},{7,5},{8,10},{10,8},{12,... | collective-permute-start | bytes 1081352 | tf_op jit(solution)/shard_map/ppermute | solution.py:244
  2.7 13.2 %collective-permute-start.3 = (bf16[4,352,128]{2,1,0:T(8,128)(2,1)S(1)}, bf16[4,352,128]{2,1,0:T(8,128)(2,1)S(1)}, u32[]{:S(2)}, u32[]{:S(2)}) collective-permute-start(bf16[4,352,128]{2,1,0:T(8,128)(2,1)S(1)} %slice.53.refs_5_.refs_9_), channel_id=1, source_target_pairs={{2,4},{4,2},{3,5},{5,3},{10,12},{12,10},{11,13},{13,11},{18,20},{2... | collective-permute-start | bytes 1081352 | tf_op jit(solution)/shard_map/ppermute | solution.py:244
  4.7 4.6 %copy-start.1 = (bf16[2,256,128]{2,1,0:T(8,128)(2,1)S(1)}, bf16[2,256,128]{2,1,0:T(8,128)(2,1)}, u32[]{:S(2)}) copy-start(bf16[2,256,128]{2,1,0:T(8,128)(2,1)} %param.11) | copy-start | bytes 393220
  5.3 5.4 %copy-start.2 = (bf16[2,128,256]{2,1,0:T(8,128)(2,1)S(1)}, bf16[2,128,256]{2,1,0:T(8,128)(2,1)}, u32[]{:S(2)}) copy-start(bf16[2,128,256]{2,1,0:T(8,128)(2,1)} %param.10) | copy-start | bytes 393220
  5.3 14.8 %collective-permute-start = (bf16[4,224,128]{2,1,0:T(8,128)(2,1)S(1)}, bf16[4,224,128]{2,1,0:T(8,128)(2,1)S(1)}, u32[]{:S(2)}, u32[]{:S(2)}) collective-permute-start(bf16[4,224,128]{2,1,0:T(8,128)(2,1)S(1)} %get-tuple-element.14.refs_5_), channel_id=1, source_target_pairs={{0,2},{2,0},{4,6},{6,4},{1,3},{3,1},{5,7},{7,5},{8,10},{10,8},{12,... | collective-permute-start | bytes 688136 | tf_op jit(solution)/shard_map/ppermute | solution.py:244
  5.4 14.7 %collective-permute-start.1 = (bf16[4,224,128]{2,1,0:T(8,128)(2,1)S(1)}, bf16[4,224,128]{2,1,0:T(8,128)(2,1)S(1)}, u32[]{:S(2)}, u32[]{:S(2)}) collective-permute-start(bf16[4,224,128]{2,1,0:T(8,128)(2,1)S(1)} %get-tuple-element.14.refs_5_), channel_id=1, source_target_pairs={{2,4},{4,2},{3,5},{5,3},{10,12},{12,10},{11,13},{13,11},{18,20},{2... | collective-permute-start | bytes 688136 | tf_op jit(solution)/shard_map/ppermute | solution.py:244
  9.3 0.7 %copy-start.4 = (bf16[2,9,128]{2,0,1:T(2,128)(2,1)S(1)}, bf16[2,9,128]{2,0,1:T(2,128)(2,1)}, u32[]{:S(2)}) copy-start(bf16[2,9,128]{2,0,1:T(2,128)(2,1)} %param.8) | copy-start | bytes 13828
  10.0 0.7 %copy-start.5 = (f32[2,128]{1,0:T(2,128)S(1)}, f32[2,128]{1,0:T(2,128)}, u32[]{:S(2)}) copy-start(f32[2,128]{1,0:T(2,128)} %param.9) | copy-start | bytes 3076
  18.1 9.9 %collective-permute-start.6 = (bf16[4,320,128]{2,1,0:T(8,128)(2,1)S(1)}, bf16[4,320,128]{2,1,0:T(8,128)(2,1)S(1)}, u32[]{:S(2)}, u32[]{:S(2)}) collective-permute-start(bf16[4,320,128]{2,1,0:T(8,128)(2,1)S(1)} %get-tuple-element.19.state.refs_5_.refs_9_), channel_id=1, source_target_pairs={{0,2},{2,0},{4,6},{6,4},{1,3},{3,1},{5,7},{7,5},{8,10},{10,8},{12,... | collective-permute-start | bytes 983048 | tf_op jit(solution)/shard_map/ppermute | solution.py:244
  18.2 11.8 %collective-permute-start.7 = (bf16[4,320,128]{2,1,0:T(8,128)(2,1)S(1)}, bf16[4,320,128]{2,1,0:T(8,128)(2,1)S(1)}, u32[]{:S(2)}, u32[]{:S(2)}) collective-permute-start(bf16[4,320,128]{2,1,0:T(8,128)(2,1)S(1)} %get-tuple-element.19.state.refs_5_.refs_9_), channel_id=1, source_target_pairs={{2,4},{4,2},{3,5},{5,3},{10,12},{12,10},{11,13},{13,11},{18,20},{2... | collective-permute-start | bytes 983048 | tf_op jit(solution)/shard_map/ppermute | solution.py:244
  21.8 10.8 %collective-permute-start.4 = (bf16[4,256,128]{2,1,0:T(8,128)(2,1)S(1)}, bf16[4,256,128]{2,1,0:T(8,128)(2,1)S(1)}, u32[]{:S(2)}, u32[]{:S(2)}) collective-permute-start(bf16[4,256,128]{2,1,0:T(8,128)(2,1)S(1)} %shard_map.66.state.refs_5_), channel_id=1, source_target_pairs={{0,2},{2,0},{4,6},{6,4},{1,3},{3,1},{5,7},{7,5},{8,10},{10,8},{12,... | collective-permute-start | bytes 786440 | tf_op jit(solution)/shard_map/ppermute | solution.py:244
  22.6 10.1 %collective-permute-start.5 = (bf16[4,256,128]{2,1,0:T(8,128)(2,1)S(1)}, bf16[4,256,128]{2,1,0:T(8,128)(2,1)S(1)}, u32[]{:S(2)}, u32[]{:S(2)}) collective-permute-start(bf16[4,256,128]{2,1,0:T(8,128)(2,1)S(1)} %shard_map.66.state.refs_5_), channel_id=1, source_target_pairs={{2,4},{4,2},{3,5},{5,3},{10,12},{12,10},{11,13},{13,11},{18,20},{2... | collective-permute-start | bytes 786440 | tf_op jit(solution)/shard_map/ppermute | solution.py:244

commit v7 on v6

--- a/solution.py
+++ b/solution.py
@@ -12,7 +12,8 @@
 TAPS = 9
 REACH = TAPS // 2
 PAD = 16
-TILE = 32
+TILE = 48
+NORM_TILE = 32
 ERFC_POWER = (
     -1.000037622280944,
     -1.1507878529643598,
@@ -87,10 +88,10 @@
         tail = refs.pop(0)
     if first and not last:
         head = refs.pop(0)
-    mix, state = refs[:2]
+    mix, state, normed = refs[:3]
     whole = out
     if place is not None:
-        out, sems = refs[2:]
+        out, sems = refs[3:]
     rows = own.shape[0]
     channels = own.shape[2]
     start = 0 if first else 2 * PAD
@@ -139,27 +140,36 @@
     scale = gain[...]
     made, total = out.shape[1], whole.shape[1]
 
-    def rest(at, tile):
+    def norm_tile(t, carry):
+        at = t * NORM_TILE
         parts = []
         for r in range(rows):
-            lon = mix[r, pl.ds(at + PAD - DLON * REACH, tile)] * lon_tap[0]
+            lon = mix[r, pl.ds(at + PAD - DLON * REACH, NORM_TILE)] * lon_tap[0]
             for k in range(1, TAPS):
-                lon = lon + mix[r, pl.ds(at + PAD + DLON * (k - REACH), tile)] * lon_tap[k]
+                lon = lon + mix[r, pl.ds(at + PAD + DLON * (k - REACH), NORM_TILE)] * lon_tap[k]
             parts.append(lon)
         lon = jnp.concatenate(parts, axis=0)
         mean = jnp.mean(lon, axis=-1, keepdims=True)
         centred = lon - mean
         var = jnp.mean(centred * centred, axis=-1, keepdims=True)
-        normed = (centred * lax.rsqrt(var + 1e-06) * scale).astype(jnp.bfloat16)
-        hidden = jnp.dot(normed, w_in[...], preferred_element_type=jnp.float32)
+        unit = (centred * lax.rsqrt(var + 1e-06) * scale).astype(jnp.bfloat16)
+        for r in range(rows):
+            normed[r, pl.ds(pl.multiple_of(at, NORM_TILE), NORM_TILE)] = unit[r * NORM_TILE : (r + 1) * NORM_TILE]
+        return carry
+
+    lax.fori_loop(0, made // NORM_TILE, norm_tile, 0)
+
+    def rest(at, tile):
+        flat = jnp.concatenate([normed[r, at : at + tile] for r in range(rows)], axis=0)
+        hidden = jnp.dot(flat, w_in[...], preferred_element_type=jnp.float32)
         hidden = gelu(hidden).astype(jnp.bfloat16)
         delta = jnp.dot(hidden, w_out[...], preferred_element_type=jnp.float32)
         for r in range(rows):
-            new = state[r, pl.ds(at + PAD, tile)].astype(jnp.float32) + delta[r * tile : (r + 1) * tile]
-            out[r, pl.ds(at, tile)] = new.astype(jnp.bfloat16)
+            new = state[r, at + PAD : at + PAD + tile].astype(jnp.float32) + delta[r * tile : (r + 1) * tile]
+            out[r, at : at + tile] = new.astype(jnp.bfloat16)
 
     copies = []
-    for at, tile in tiles(made):
+    for at, tile in tiles(made, total, place):
         rest(at, tile)
         if place is not None:
             to = (place + at) % total
@@ -171,8 +181,12 @@
         copy.wait()
 
 
-def tiles(made):
-    return [(at, min(TILE, made - at)) for at in range(0, made, TILE)]
+def tiles(made, total, place):
+    edges = set(range(0, made, TILE)) | {made}
+    if place is not None and place + made > total:
+        edges = set(range(0, total - place, TILE)) | set(range(total - place, made, TILE)) | {made}
+    edges = sorted(edges)
+    return [(lo, hi - lo) for lo, hi in zip(edges[:-1], edges[1:])]
 
 
 def layer_chunk(bands, weights, chunk, prev, first_chunk, first, last, place=None, whole=None):
@@ -192,11 +206,13 @@
     scratch = [
         pltpu.VMEM((rows, window, channels), jnp.float32),
         pltpu.VMEM((rows, window, channels), jnp.bfloat16),
+        pltpu.VMEM((rows, made, channels), jnp.bfloat16),
     ]
     aliases = {}
     if place is not None:
-        scratch += [pltpu.VMEM(outs[0].shape, jnp.bfloat16), pltpu.SemaphoreType.DMA((len(tiles(made)),))]
-        outs = [jax.ShapeDtypeStruct((rows, whole if first else whole.shape[1], channels), jnp.bfloat16)]
+        lons = whole if first else whole.shape[1]
+        scratch += [pltpu.VMEM(outs[0].shape, jnp.bfloat16), pltpu.SemaphoreType.DMA((len(tiles(made, lons, place)),))]
+        outs = [jax.ShapeDtypeStruct((rows, lons, channels), jnp.bfloat16)]
         out_specs = [pl.BlockSpec(memory_space=pltpu.HBM)]
         if not first:
             aliases = {len(args): 0}
@@ -224,7 +240,7 @@
 
 
 def splits(total):
-    first = PAD * ((total // PAD + 4 * LAYERS) // 2)
+    first = 2 * PAD * ((total // PAD + 2 * LAYERS) // 4)
     return [(0, first), (first, total)]
 
 

time: 35.5 us -> 38.6 us (1.087)
  the two profiles are of different devices: /device:TPU:18 before, /device:TPU:14 now
where the time goes in v7:
time: 38.6 us; the launch traced here: 38.4 us
  Pallas kernels  15.6 us (40%)
  starting transfers between devices  13.9 us (36%)
  waiting for transfers between devices  6.15 us (16%)
  local copies, waits for them, and re-layouts  2.47 us (6%)
    pallas_call x4, Pallas kernels, layer_chunk(): pl.pallas_call(functools.partial(chunk_kernel, bands, first, last, width,...  14.5 us
    ppermute x4, starting transfers between devices, member_step(): lax.ppermute(own, 'band', odd_pairs)  13.1 us
    ppermute x4, waiting for transfers between devices, member_step(): lax.ppermute(own, 'band', odd_pairs)  4.7 us
    ppermute x4, waiting for transfers between devices, member_step(): lax.ppermute(own, 'band', even_pairs)  1.46 us
    unnamed x12, local copies, waits for them, and re-layouts  1.35 us
    pallas_call x3, Pallas kernels, own_share(): pl.pallas_call(functools.partial(own_kernel, ranges), out_shape=shapes, i...  1.09 us
    slice x1, local copies, waits for them, and re-layouts, member_step(): chunks = [state[:, :ranges[0][1]]] + later  1.07 us
  transfers between devices with their start and end apart: 8, of which 3 were waited for; matrix products, arithmetic and copies ran while one was open for 0% of the time, Pallas kernels for 29%

profile of v7, /device:TPU:14, one launch (start us, length us, event | category | flops | bytes accessed | tf_op | source)
XLA Modules:
  0.0 38.4 jit_solution(4876791501434825055)
XLA Ops:
  0.0 1.1 %slice.53.refs_5_.refs_9_ = bf16[4,320,128]{2,1,0:T(8,128)(2,1)S(1)} slice(bf16[4,576,128]{2,1,0:T(8,128)(2,1)} %bitcast.30), slice={[0:4], [0:320], [0:128]} | slice | bytes 655360 | tf_op jit(solution)/shard_map/slice | solution.py:257
  1.1 0.5 %collective-permute-start.2 = (bf16[4,320,128]{2,1,0:T(8,128)(2,1)S(1)}, bf16[4,320,128]{2,1,0:T(8,128)(2,1)S(1)}, u32[]{:S(2)}, u32[]{:S(2)}) collective-permute-start(bf16[4,320,128]{2,1,0:T(8,128)(2,1)S(1)} %slice.53.refs_5_.refs_9_), channel_id=1, source_target_pairs={{0,2},{2,0},{4,6},{6,4},{1,3},{3,1},{5,7},{7,5},{8,10},{10,8},{12,... | collective-permute-start | bytes 983048 | tf_op jit(solution)/shard_map/ppermute | solution.py:260
  1.6 4.6 %collective-permute-start.3 = (bf16[4,320,128]{2,1,0:T(8,128)(2,1)S(1)}, bf16[4,320,128]{2,1,0:T(8,128)(2,1)S(1)}, u32[]{:S(2)}, u32[]{:S(2)}) collective-permute-start(bf16[4,320,128]{2,1,0:T(8,128)(2,1)S(1)} %slice.53.refs_5_.refs_9_), channel_id=1, source_target_pairs={{2,4},{4,2},{3,5},{5,3},{10,12},{12,10},{11,13},{13,11},{18,20},{2... | collective-permute-start | bytes 983048 | tf_op jit(solution)/shard_map/ppermute | solution.py:260
  6.3 0.0 copy-start.1
  6.3 0.6 %shard_map.64 = (f32[4,320,128]{2,1,0:T(8,128)S(1)}, f32[4,256,128]{2,1,0:T(8,128)S(1)}, bf16[4,256,128]{2,1,0:T(8,128)(2,1)S(1)}) custom-call(f32[9,128]{1,0:T(8,128)S(1)} %fusion.1.lat_w.refs_0_, bf16[4,576,128]{2,1,0:T(8,128)(2,1)S(1)} %bitcast.31), custom_call_target="tpu_custom_call" | custom-call | flops 943718400 | bytes 2359296 | tf_op jit(solution)/shard_map/pallas_call | solution.py:61
  6.8 0.0 copy-start.2
  6.8 0.1 collective-permute-start
  6.9 1.9 %collective-permute-start.1 = (bf16[4,256,128]{2,1,0:T(8,128)(2,1)S(1)}, bf16[4,256,128]{2,1,0:T(8,128)(2,1)S(1)}, u32[]{:S(2)}, u32[]{:S(2)}) collective-permute-start(bf16[4,256,128]{2,1,0:T(8,128)(2,1)S(1)} %get-tuple-element.14.refs_5_), channel_id=1, source_target_pairs={{2,4},{4,2},{3,5},{5,3},{10,12},{12,10},{11,13},{13,11},{18,20},{2... | collective-permute-start | bytes 786440 | tf_op jit(solution)/shard_map/ppermute | solution.py:260
  8.9 0.0 copy-start.4
  8.9 0.7 %copy-done.4 = bf16[2,9,128]{2,0,1:T(2,128)(2,1)S(1)} copy-done((bf16[2,9,128]{2,0,1:T(2,128)(2,1)S(1)}, bf16[2,9,128]{2,0,1:T(2,128)(2,1)}, u32[]{:S(2)}) %copy-start.4) | copy-done | bytes 4632
  9.6 0.7 %copy-done.5 = f32[2,128]{1,0:T(2,128)S(1)} copy-done((f32[2,128]{1,0:T(2,128)S(1)}, f32[2,128]{1,0:T(2,128)}, u32[]{:S(2)}) %copy-start.5) | copy-done | bytes 1048
  10.3 1.4 %collective-permute-done.2.refs_7_ = bf16[4,320,128]{2,1,0:T(8,128)(2,1)S(1)} collective-permute-done((bf16[4,320,128]{2,1,0:T(8,128)(2,1)S(1)}, bf16[4,320,128]{2,1,0:T(8,128)(2,1)S(1)}, u32[]{:S(2)}, u32[]{:S(2)}) %collective-permute-start.2) | collective-permute-done | bytes 327712 | tf_op jit(solution)/shard_map/ppermute | solution.py:260
  11.7 3.0 %collective-permute-done.3.refs_8_ = bf16[4,320,128]{2,1,0:T(8,128)(2,1)S(1)} collective-permute-done((bf16[4,320,128]{2,1,0:T(8,128)(2,1)S(1)}, bf16[4,320,128]{2,1,0:T(8,128)(2,1)S(1)}, u32[]{:S(2)}, u32[]{:S(2)}) %collective-permute-start.3) | collective-permute-done | bytes 327712 | tf_op jit(solution)/shard_map/ppermute | solution.py:260
  14.8 3.3 %shard_map.65 = (bf16[4,288,128]{2,1,0:T(8,128)(2,1)S(1)}, bf16[4,32,128]{2,1,0:T(8,128)(2,1)S(1)}, bf16[4,32,128]{2,1,0:T(8,128)(2,1)S(1)}) custom-call(f32[9,128]{1,0:T(8,128)S(1)} %fusion.1.lat_w.refs_0_, f32[9,128]{1,0:T(8,128)S(1)} %fusion.refs_1_, f32[1,128]{1,0:T(1,128)S(1)} %get-tuple-element.31.refs_2_, ...), custom_call_target="tpu_custom_call" | custom-call | flops 1887436800 | bytes 1179648 | tf_op jit(solution)/shard_map/pallas_call | solution.py:228
  18.1 0.1 collective-permute-start.6
  18.2 4.0 %collective-permute-start.7 = (bf16[4,288,128]{2,1,0:T(8,128)(2,1)S(1)}, bf16[4,288,128]{2,1,0:T(8,128)(2,1)S(1)}, u32[]{:S(2)}, u32[]{:S(2)}) collective-permute-start(bf16[4,288,128]{2,1,0:T(8,128)(2,1)S(1)} %get-tuple-element.19.state.refs_5_.refs_9_), channel_id=1, source_target_pairs={{2,4},{4,2},{3,5},{5,3},{10,12},{12,10},{11,13},{13,11},{18,20},{2... | collective-permute-start | bytes 884744 | tf_op jit(solution)/shard_map/ppermute | solution.py:260
  22.2 3.2 %shard_map.66.state.refs_5_ = bf16[4,288,128]{2,1,0:T(8,128)(2,1)S(1)} custom-call(f32[9,128]{1,0:T(8,128)S(1)} %fusion.1.lat_w.refs_0_, f32[9,128]{1,0:T(8,128)S(1)} %fusion.refs_1_, f32[1,128]{1,0:T(1,128)S(1)} %get-tuple-element.31.refs_2_, bf16[128,256]{1,0:T(8,128)(2,1)S(1)} %get-tuple-element.25.refs_3_, ...), custom_call_target="tpu_custom_call" | custom-call | flops 1887436800 | bytes 1179648 | tf_op jit(solution)/shard_map/pallas_call | solution.py:228
  25.4 0.1 collective-permute-start.4
  25.5 2.7 %collective-permute-start.5 = (bf16[4,288,128]{2,1,0:T(8,128)(2,1)S(1)}, bf16[4,288,128]{2,1,0:T(8,128)(2,1)S(1)}, u32[]{:S(2)}, u32[]{:S(2)}) collective-permute-start(bf16[4,288,128]{2,1,0:T(8,128)(2,1)S(1)} %shard_map.66.state.refs_5_), channel_id=1, source_target_pairs={{2,4},{4,2},{3,5},{5,3},{10,12},{12,10},{11,13},{13,11},{18,20},{2... | collective-permute-start | bytes 884744 | tf_op jit(solution)/shard_map/ppermute | solution.py:260
  28.2 0.3 shard_map.68.refs_6_
  28.4 0.3 shard_map.67.refs_6_
  28.7 3.7 %shard_map.69 = (bf16[4,576,128]{2,1,0:T(8,128)(2,1)}, bf16[4,32,128]{2,1,0:T(8,128)(2,1)S(1)}, bf16[4,32,128]{2,1,0:T(8,128)(2,1)S(1)}) custom-call(f32[9,128]{1,0:T(8,128)S(1)} %get-tuple-element.34.lat_w.refs_0_, f32[9,128]{1,0:T(8,128)S(1)} %get-tuple-element.33.refs_1_, f32[1,128]{1,0:T(1,128)S(1)} %get-tuple-element.32.refs_2_, ...), custom_call_target="tpu_custom_call" | custom-call | flops 1677721600 | bytes 1048576 | tf_op jit(solution)/shard_map/pallas_call | solution.py:228
  32.4 1.7 %collective-permute-done.5.refs_8_ = bf16[4,288,128]{2,1,0:T(8,128)(2,1)S(1)} collective-permute-done((bf16[4,288,128]{2,1,0:T(8,128)(2,1)S(1)}, bf16[4,288,128]{2,1,0:T(8,128)(2,1)S(1)}, u32[]{:S(2)}, u32[]{:S(2)}) %collective-permute-start.5) | collective-permute-done | bytes 294944 | tf_op jit(solution)/shard_map/ppermute | solution.py:260
  34.1 4.3 %shard_map.70 = bf16[4,576,128]{2,1,0:T(8,128)(2,1)} custom-call(f32[9,128]{1,0:T(8,128)S(1)} %get-tuple-element.34.lat_w.refs_0_, f32[9,128]{1,0:T(8,128)S(1)} %get-tuple-element.33.refs_1_, f32[1,128]{1,0:T(1,128)S(1)} %get-tuple-element.32.refs_2_, bf16[128,256]{1,0:T(8,128)(2,1)S(1)} %get-tuple-element.26.refs_3_, ...), custom_call_target="tpu_custom_call", output_to_operand_aliasing={{}: (13, {})} | custom-call | flops 2097152000 | bytes 1310720 | tf_op jit(solution)/shard_map/pallas_call | solution.py:228
  (22 shorter events, 0.1 us)
Async XLA Ops:
  0.0 6.2 %copy-start = (bf16[1,4,576,128]{3,2,1,0:T(8,128)(2,1)S(1)}, bf16[1,4,576,128]{3,2,1,0:T(8,128)(2,1)}, u32[]{:S(2)}) copy-start(bf16[1,4,576,128]{3,2,1,0:T(8,128)(2,1)} %param.6) | copy-start | bytes 1769476
  0.0 6.2 %copy-start.3 = (bf16[2,9,128]{2,0,1:T(2,128)(2,1)S(1)}, bf16[2,9,128]{2,0,1:T(2,128)(2,1)}, u32[]{:S(2)}) copy-start(bf16[2,9,128]{2,0,1:T(2,128)(2,1)} %param.7) | copy-start | bytes 13828
  1.1 10.7 %collective-permute-start.2 = (bf16[4,320,128]{2,1,0:T(8,128)(2,1)S(1)}, bf16[4,320,128]{2,1,0:T(8,128)(2,1)S(1)}, u32[]{:S(2)}, u32[]{:S(2)}) collective-permute-start(bf16[4,320,128]{2,1,0:T(8,128)(2,1)S(1)} %slice.53.refs_5_.refs_9_), channel_id=1, source_target_pairs={{0,2},{2,0},{4,6},{6,4},{1,3},{3,1},{5,7},{7,5},{8,10},{10,8},{12,... | collective-permute-start | bytes 983048 | tf_op jit(solution)/shard_map/ppermute | solution.py:260
  1.6 13.2 %collective-permute-start.3 = (bf16[4,320,128]{2,1,0:T(8,128)(2,1)S(1)}, bf16[4,320,128]{2,1,0:T(8,128)(2,1)S(1)}, u32[]{:S(2)}, u32[]{:S(2)}) collective-permute-start(bf16[4,320,128]{2,1,0:T(8,128)(2,1)S(1)} %slice.53.refs_5_.refs_9_), channel_id=1, source_target_pairs={{2,4},{4,2},{3,5},{5,3},{10,12},{12,10},{11,13},{13,11},{18,20},{2... | collective-permute-start | bytes 983048 | tf_op jit(solution)/shard_map/ppermute | solution.py:260
  6.3 2.6 %copy-start.1 = (bf16[2,256,128]{2,1,0:T(8,128)(2,1)S(1)}, bf16[2,256,128]{2,1,0:T(8,128)(2,1)}, u32[]{:S(2)}) copy-start(bf16[2,256,128]{2,1,0:T(8,128)(2,1)} %param.11) | copy-start | bytes 393220
  6.8 2.1 %copy-start.2 = (bf16[2,128,256]{2,1,0:T(8,128)(2,1)S(1)}, bf16[2,128,256]{2,1,0:T(8,128)(2,1)}, u32[]{:S(2)}) copy-start(bf16[2,128,256]{2,1,0:T(8,128)(2,1)} %param.10) | copy-start | bytes 393220
  6.8 15.3 %collective-permute-start = (bf16[4,256,128]{2,1,0:T(8,128)(2,1)S(1)}, bf16[4,256,128]{2,1,0:T(8,128)(2,1)S(1)}, u32[]{:S(2)}, u32[]{:S(2)}) collective-permute-start(bf16[4,256,128]{2,1,0:T(8,128)(2,1)S(1)} %get-tuple-element.14.refs_5_), channel_id=1, source_target_pairs={{0,2},{2,0},{4,6},{6,4},{1,3},{3,1},{5,7},{7,5},{8,10},{10,8},{12,... | collective-permute-start | bytes 786440 | tf_op jit(solution)/shard_map/ppermute | solution.py:260
  6.9 15.2 %collective-permute-start.1 = (bf16[4,256,128]{2,1,0:T(8,128)(2,1)S(1)}, bf16[4,256,128]{2,1,0:T(8,128)(2,1)S(1)}, u32[]{:S(2)}, u32[]{:S(2)}) collective-permute-start(bf16[4,256,128]{2,1,0:T(8,128)(2,1)S(1)} %get-tuple-element.14.refs_5_), channel_id=1, source_target_pairs={{2,4},{4,2},{3,5},{5,3},{10,12},{12,10},{11,13},{13,11},{18,20},{2... | collective-permute-start | bytes 786440 | tf_op jit(solution)/shard_map/ppermute | solution.py:260
  8.9 0.7 %copy-start.4 = (bf16[2,9,128]{2,0,1:T(2,128)(2,1)S(1)}, bf16[2,9,128]{2,0,1:T(2,128)(2,1)}, u32[]{:S(2)}) copy-start(bf16[2,9,128]{2,0,1:T(2,128)(2,1)} %param.8) | copy-start | bytes 13828
  9.6 0.7 %copy-start.5 = (f32[2,128]{1,0:T(2,128)S(1)}, f32[2,128]{1,0:T(2,128)}, u32[]{:S(2)}) copy-start(f32[2,128]{1,0:T(2,128)} %param.9) | copy-start | bytes 3076
  18.1 10.6 %collective-permute-start.6 = (bf16[4,288,128]{2,1,0:T(8,128)(2,1)S(1)}, bf16[4,288,128]{2,1,0:T(8,128)(2,1)S(1)}, u32[]{:S(2)}, u32[]{:S(2)}) collective-permute-start(bf16[4,288,128]{2,1,0:T(8,128)(2,1)S(1)} %get-tuple-element.19.state.refs_5_.refs_9_), channel_id=1, source_target_pairs={{0,2},{2,0},{4,6},{6,4},{1,3},{3,1},{5,7},{7,5},{8,10},{10,8},{12,... | collective-permute-start | bytes 884744 | tf_op jit(solution)/shard_map/ppermute | solution.py:260
  18.2 10.5 %collective-permute-start.7 = (bf16[4,288,128]{2,1,0:T(8,128)(2,1)S(1)}, bf16[4,288,128]{2,1,0:T(8,128)(2,1)S(1)}, u32[]{:S(2)}, u32[]{:S(2)}) collective-permute-start(bf16[4,288,128]{2,1,0:T(8,128)(2,1)S(1)} %get-tuple-element.19.state.refs_5_.refs_9_), channel_id=1, source_target_pairs={{2,4},{4,2},{3,5},{5,3},{10,12},{12,10},{11,13},{13,11},{18,20},{2... | collective-permute-start | bytes 884744 | tf_op jit(solution)/shard_map/ppermute | solution.py:260
  25.4 7.0 %collective-permute-start.4 = (bf16[4,288,128]{2,1,0:T(8,128)(2,1)S(1)}, bf16[4,288,128]{2,1,0:T(8,128)(2,1)S(1)}, u32[]{:S(2)}, u32[]{:S(2)}) collective-permute-start(bf16[4,288,128]{2,1,0:T(8,128)(2,1)S(1)} %shard_map.66.state.refs_5_), channel_id=1, source_target_pairs={{0,2},{2,0},{4,6},{6,4},{1,3},{3,1},{5,7},{7,5},{8,10},{10,8},{12,... | collective-permute-start | bytes 884744 | tf_op jit(solution)/shard_map/ppermute | solution.py:260
  25.5 8.6 %collective-permute-start.5 = (bf16[4,288,128]{2,1,0:T(8,128)(2,1)S(1)}, bf16[4,288,128]{2,1,0:T(8,128)(2,1)S(1)}, u32[]{:S(2)}, u32[]{:S(2)}) collective-permute-start(bf16[4,288,128]{2,1,0:T(8,128)(2,1)S(1)} %shard_map.66.state.refs_5_), channel_id=1, source_target_pairs={{2,4},{4,2},{3,5},{5,3},{10,12},{12,10},{11,13},{13,11},{18,20},{2... | collective-permute-start | bytes 884744 | tf_op jit(solution)/shard_map/ppermute | solution.py:260
